TPU v7x, 32 devices: a whole 2x2x4 slice. The times are simulated.
32 devices in a mesh: section: 4 (over y, core), blk: 8 (over z, x).
Axes of the slice: x: 2, y: 2, z: 4, core: 2. Of those that a mesh axis runs over, the one named last changes fastest.
Arguments:
- residual: float32 [1536, 32, 128], P(('section', 'blk')), may hold values from -6 to 6
- kin_inverse: float32 [1536, 32, 32], P(('section', 'blk'))
- cell_weight: float32 [1536, 128], P(('section', 'blk')), may hold values from 0.5 to 1
- upwind_frac: float32 [1536, 4, 128], P(('section', 'blk')), may hold values from 0.2 to 0.7
- block_level: int32 [1536], P(('section', 'blk')), may hold values from 0 to 5, as said below
- send_in: int32 [32, 5, 8], P(('section', 'blk')), may hold values from 0 to 48, as said below
- send_down: int32 [32, 5, 8], P(('section', 'blk')), may hold values from 0 to 48, as said below
- upwind_slot: int32 [1536, 4], P(('section', 'blk')), may hold values from 0 to 128, as said below
Outputs:
- newton_step: float32 [1536, 32, 128], P(('section', 'blk'))
Inputs may be any that keep to these rules, and one draw needn't show every extreme that they name: `block_level`: on each device the blocks of levels 0 to 5 number 48 * 8 / 24, 6 / 24, 4 / 24, 3 / 24, 2 / 24 and 1 / 24 in some cyclic order of the levels, so one level holds 16 blocks of every device. `send_in`: an entry other than 48 names a block of level l on the sending device, for entry [d, l, i]. About half of the entries are none; for every section and level some device receives a block from every device of its section. `send_down`: as send_in, for the owner i of the next section. The last section sends none; for every other section and level some device of the next section receives a block from every device of the sending section. `upwind_slot`: every source of a block has a lower level than the block (a slot of send level l counts as level l), and a slot that is named holds a block; blocks of level 0 have none.
All inputs are finite; a program needn't handle non-finite values.
Results may differ from a plain program's by a relative error of at most 0.0001.
Values sent between devices are 32-bit elements; how exact they have to be, the bound alone decides.
No kernel may reach another device: no remote copies, remote signals or barrier semaphores. Data moves between devices by JAX's collectives and lax.ppermute only.
A program may use at most 64 MiB of HBM per device.

v0:
```python
import functools

import jax
import jax.numpy as jnp
from jax import lax
from jax.experimental import pallas as pl
from jax.experimental.pallas import tpu as pltpu
from jax.sharding import PartitionSpec as P


def split_of(groups):
    columns = max(c for c in range(1, groups + 1) if groups % c == 0 and c * c <= groups)
    return groups // columns, columns


def stepped(row, step, rows, back=False):
    if rows & (rows - 1) == 0:
        return row ^ step
    return (row + (rows - step if back else step)) % rows


def moved(value, sections, rows, columns, steps):
    groups = rows * columns
    pairs = []
    for section in range(sections):
        for row in range(rows):
            for column in range(columns):
                target = stepped(row, steps[1], rows) * columns + (column + steps[2]) % columns
                below = (section + steps[0]) % sections
                pairs.append((section * groups + row * columns + column, below * groups + target))
    return lax.ppermute(value, ("section", "blk"), pairs)


def halves_of(rows):
    return rows // 2 if rows > 1 and rows & (rows - 1) == 0 else rows


def wrapped(value, count):
    return jnp.where(value >= count, value - count, value)


def sort_blocks(blocks, levels, plan):
    stride = blocks + 1
    count = plan.shape[0] // stride
    together = 4 if blocks % 4 == 0 else 1

    def place(step, ends):
        for i in range(together):
            block = step * together + i
            level = levels[block]
            for end in ends:
                plan[end] = block
            ends = tuple(end + jnp.where(level == own, 1, 0) for own, end in enumerate(ends))
        return ends

    ends = lax.fori_loop(0, blocks // together, place, tuple(jnp.int32(own * stride) for own in range(count)))
    for own, end in enumerate(ends):
        plan[own * stride + blocks] = end - own * stride


def solve_blocks(level, blocks, plan, inflow_of, kin, weight, pool):
    first = level * (blocks + 1)
    count = plan[first + blocks]
    ids = [plan[first + jnp.minimum(i, count - 1)] for i in range(blocks * 8 // 24)]
    solved = []
    for block in ids:
        mixed = jnp.dot(
            kin[block], inflow_of(block), precision=lax.Precision.HIGH, preferred_element_type=jnp.float32
        )
        solved.append(weight[pl.ds(block, 1), :] * mixed)
    for block, value in zip(ids, solved):
        pool[block] = value


def fill_sends(level, rows, columns, blocks, peers, downs, pool, outs):
    here = lax.axis_index("blk")
    row, column = here // columns, lax.rem(here, columns)
    ends = lax.axis_index("section") == lax.axis_size("section") - 1
    half = halves_of(rows)
    for row_step in range(rows):
        to_row = stepped(row, row_step, rows)
        for column_step in range(columns):
            target = to_row * columns + wrapped(column + column_step, columns)
            outs[columns - 1 + column_step][row_step] = pool[jnp.where(ends, blocks, downs[level, 0, target])]
            peer = pool[peers[level, 0, target]]
            if column_step:
                outs[column_step - 1][row_step] = peer
            else:
                outs[2 * columns - 1 + row_step // half][row_step % half] = peer


def first_level(rows, columns, *refs):
    refs = list(refs)
    levels_in, kin_in, residual_in, weight_in, peers_in, downs_in, slots_in, frac_in = (refs.pop(0) for _ in range(8))
    pool, kin, plan_out, peers_out, downs_out, slots_out, residual, weight, frac = (refs.pop(0) for _ in range(9))
    outs = [refs.pop(0) for _ in range(2 * columns - 1 + rows // halves_of(rows))]
    plan, levels, kin_here, peers, downs, sems = refs
    pairs = [(levels_in, levels), (kin_in, kin_here), (residual_in, residual), (weight_in, weight)]
    pairs += [(peers_in, peers), (downs_in, downs)]
    pairs += [(peers_in, peers_out), (downs_in, downs_out), (slots_in, slots_out), (frac_in, frac)]
    pairs += [(plan, plan_out)]
    copies = [pltpu.make_async_copy(source, target, sems.at[i]) for i, (source, target) in enumerate(pairs)]
    for copy in copies[:-1]:
        copy.start()
    blocks = residual.shape[0]
    pool[blocks] = jnp.zeros(pool.shape[1:], pool.dtype)
    copies[0].wait()
    sort_blocks(blocks, levels, plan)
    copies[-1].start()
    copies[1].wait()
    for i in range(kin.shape[1]):
        kin[:, i, :] = jnp.transpose(kin_here[i])
    for copy in copies[2:6]:
        copy.wait()

    solve_blocks(0, blocks, plan, lambda block: residual[block], kin, weight, pool)
    fill_sends(0, rows, columns, blocks, peers, downs, pool, outs)
    for copy in copies[6:]:
        copy.wait()


def later_level(level, rows, columns, plan, peers, downs, slots, residual, weight, frac, kin, *refs):
    refs = list(refs)
    half = halves_of(rows)
    from_above = [refs.pop(0) for _ in range(columns)]
    over_columns = [None] + [refs.pop(0) for _ in range(1, columns)]
    own_column = [refs.pop(0) for _ in range(rows // half)]
    arrived = {step: refs.pop(0) for step in range(rows - 1, 0, -1)}
    refs.pop(0)
    pool = refs.pop(0)
    outs = refs
    blocks, upw = residual.shape[0], slots.shape[0]
    rounds, groups = peers.shape[0], rows * columns
    here = lax.axis_index("blk")
    row, column = here // columns, lax.rem(here, columns)
    peers_first = blocks + 1 + (level - 1) * groups
    downs_first = peers_first + rounds * groups
    for row_step in range(rows):
        from_row = stepped(row, row_step, rows, back=True)
        for column_step in range(columns):
            source = from_row * columns + wrapped(column + columns - column_step, columns)
            down = arrived[row_step].at[columns - 1 + column_step] if row_step else from_above[column_step].at[0]
            if column_step:
                peer = arrived[row_step].at[column_step - 1] if row_step else over_columns[column_step].at[0]
            else:
                at, rest = row_step // half, row_step % half
                peer = arrived[rest].at[2 * columns - 1 + at] if rest else own_column[at].at[0]
            pool[downs_first + source] = down[...]
            pool[peers_first + source] = peer[...]

    def inflow_of(block):
        inflow = residual[block]
        parts = frac[block]
        for k in range(upw):
            inflow = inflow + parts[k : k + 1, :] * pool[slots[k, block]]
        return inflow

    solve_blocks(level, blocks, plan, inflow_of, kin, weight, pool)
    if level < rounds:
        fill_sends(level, rows, columns, blocks, peers, downs, pool, outs)
    else:
        outs[0][...] = pool[pl.ds(0, blocks)]


def shards(
    residual, kin_inverse, cell_weight, upwind_frac, block_level, send_in, send_down, upwind_slot
):
    blocks, species, cells = residual.shape
    sections, groups = lax.axis_size("section"), lax.axis_size("blk")
    rows, columns = split_of(groups)
    rounds = send_in.shape[1]
    peers = send_in.transpose(1, 0, 2)
    downs = send_down.transpose(1, 0, 2)
    slots = upwind_slot.transpose(1, 0)
    kin_turned = kin_inverse.transpose(1, 2, 0)
    smem = pl.BlockSpec(memory_space=pltpu.SMEM)
    vmem = pl.BlockSpec(memory_space=pltpu.VMEM)
    hbm = pl.BlockSpec(memory_space=pltpu.HBM)
    params = pltpu.CompilerParams(vmem_limit_bytes=40 * 1024 * 1024)
    pool_shape = jax.ShapeDtypeStruct((blocks + 1 + 2 * rounds * groups, species, cells), jnp.float32)
    kin_shape = jax.ShapeDtypeStruct((blocks, species, species), jnp.float32)
    half = halves_of(rows)
    send_shapes = [jax.ShapeDtypeStruct((rows, species, cells), jnp.float32)] * (2 * columns - 1)
    send_shapes += [jax.ShapeDtypeStruct((half, species, cells), jnp.float32)] * (rows // half)
    to_first = (block_level, kin_turned, residual, cell_weight, peers, downs, slots, upwind_frac)
    held = (peers, downs, slots, residual, cell_weight, upwind_frac)
    held_shapes = [jax.ShapeDtypeStruct(((rounds + 1) * (blocks + 1),), jnp.int32)]
    held_shapes += [jax.ShapeDtypeStruct(x.shape, x.dtype) for x in held]
    pool, kin, *outs = pl.pallas_call(
        functools.partial(first_level, rows, columns),
        in_specs=[hbm] * len(to_first),
        out_specs=[vmem] * (2 + len(held_shapes) + len(send_shapes)),
        out_shape=[pool_shape, kin_shape] + held_shapes + send_shapes,
        scratch_shapes=[
            pltpu.SMEM(held_shapes[0].shape, jnp.int32),
            pltpu.SMEM(block_level.shape, jnp.int32),
            pltpu.VMEM(kin_turned.shape, jnp.float32),
            pltpu.SMEM(peers.shape, jnp.int32),
            pltpu.SMEM(downs.shape, jnp.int32),
            pltpu.SemaphoreType.DMA((11,)),
        ],
        compiler_params=params,
        name="first_level",
    )(*(pltpu.with_memory_space_constraint(x, pltpu.HBM) for x in to_first))
    held, outs = outs[: len(held_shapes)], outs[len(held_shapes) :]
    for level in range(1, rounds + 1):
        over_columns = [moved(outs[c - 1], sections, rows, columns, (0, 0, c)) for c in range(1, columns)]
        from_above = [moved(outs[columns - 1 + c], sections, rows, columns, (1, 0, c)) for c in range(columns)]
        over_columns, from_above = lax.optimization_barrier((over_columns, from_above))
        own_column = outs[2 * columns - 1 :]
        if half < rows:
            own_column[1] = moved(own_column[1], sections, rows, columns, (0, half, 0))
        arrived = []
        for step in range(rows - 1, 0, -1):
            part = [value[step] for value in over_columns + from_above]
            if step < half:
                part += [value[step] for value in own_column]
            arrived.append(moved(jnp.stack(part), sections, rows, columns, (0, step, 0)))
        if level < rounds:
            out_shapes = send_shapes
        else:
            out_shapes = [jax.ShapeDtypeStruct(residual.shape, residual.dtype)]
        operands = held + [kin] + from_above + over_columns + own_column + arrived + [pool]
        pool, *outs = pl.pallas_call(
            functools.partial(later_level, level, rows, columns),
            in_specs=[smem] * 4 + [vmem] * (len(operands) - 4),
            out_specs=[vmem] * (1 + len(out_shapes)),
            out_shape=[pool_shape] + out_shapes,
            input_output_aliases={len(operands) - 1: 0},
            compiler_params=params,
            name="later_level",
        )(*operands)
    return outs[0]


def solution(mesh):
    return jax.shard_map(
        shards,
        mesh=mesh,
        in_specs=(
            P(("section", "blk"), None, None),
            P(("section", "blk"), None, None),
            P(("section", "blk"), None),
            P(("section", "blk"), None, None),
            P(("section", "blk")),
            P(("section", "blk"), None, None),
            P(("section", "blk"), None, None),
            P(("section", "blk"), None),
        ),
        out_specs=P(("section", "blk"), None, None),
        check_vma=False,
    )
```

profile of v0, /device:TPU:0, one launch (start us, length us, event | category | flops | bytes accessed | tf_op | source)
XLA Modules:
  0.0 83.1 jit_solution(575604421956146174)
XLA Ops:
  0.0 2.3 %first_level.1 = (f32[129,32,128]{2,1,0:T(8,128)S(1)}, f32[48,32,32]{2,1,0:T(8,128)S(1)}, s32[294]{0:T(512)S(1)}, s32[5,1,8]{2,1,0:T(1,128)S(1)}, s32[5,1,8]{2,1...) custom-call(s32[48]{0:T(128)} %refs_0_.1, ...), custom_call_target="tpu_custom_call" | custom-call | tf_op jit(solution)/shard_map/first_level/pallas_call | solution.py:189
  2.3 3.0 %collective-permute-start = (f32[4,32,128]{2,1,0:T(8,128)S(1)}, f32[4,32,128]{2,1,0:T(8,128)S(1)}, u32[]{:S(2)}, u32[]{:S(2)}) collective-permute-start(f32[4,32,128]{2,1,0:T(8,128)S(1)} %get-tuple-element.67), channel_id=1, source_target_pairs={{0,1},{1,0},{2,3},{3,2},{4,5},{5,4},{6,7},{7,6},{8,9},{9,8},{10,11... | collective-permute-start | bytes 196616 | tf_op jit(solution)/shard_map/ppermute | solution.py:31
  5.3 1.8 %collective-permute-start.2 = (f32[4,32,128]{2,1,0:T(8,128)S(1)}, f32[4,32,128]{2,1,0:T(8,128)S(1)}, u32[]{:S(2)}, u32[]{:S(2)}) collective-permute-start(f32[4,32,128]{2,1,0:T(8,128)S(1)} %get-tuple-element.69), channel_id=1, source_target_pairs={{0,9},{1,8},{2,11},{3,10},{4,13},{5,12},{6,15},{7,14},{8,17},{9,16... | collective-permute-start | bytes 196616 | tf_op jit(solution)/shard_map/ppermute | solution.py:31
  7.0 2.6 %collective-permute-start.3 = (f32[2,32,128]{2,1,0:T(8,128)S(1)}, f32[2,32,128]{2,1,0:T(8,128)S(1)}, u32[]{:S(2)}, u32[]{:S(2)}) collective-permute-start(f32[2,32,128]{2,1,0:T(8,128)S(1)} %get-tuple-element.74), channel_id=1, source_target_pairs={{0,4},{1,5},{2,6},{3,7},{4,0},{5,1},{6,2},{7,3},{8,12},{9,13},{10,... | collective-permute-start | bytes 98312 | tf_op jit(solution)/shard_map/ppermute | solution.py:31
  9.9 3.7 %collective-permute-start.4 = (f32[3,32,128]{2,1,0:T(8,128)S(1)}, f32[3,32,128]{2,1,0:T(8,128)S(1)}, u32[]{:S(2)}, u32[]{:S(2)}) collective-permute-start(f32[3,32,128]{2,1,0:T(8,128)S(1)} %pad_maximum_fusion), channel_id=1, source_target_pairs={{0,6},{1,7},{2,4},{3,5},{4,2},{5,3},{6,0},{7,1},{8,14},{9,15},{10,... | collective-permute-start | bytes 147464 | tf_op jit(solution)/shard_map/ppermute | solution.py:31
  13.7 2.6 %collective-permute-start.5 = (f32[3,32,128]{2,1,0:T(8,128)S(1)}, f32[3,32,128]{2,1,0:T(8,128)S(1)}, u32[]{:S(2)}, u32[]{:S(2)}) collective-permute-start(f32[3,32,128]{2,1,0:T(8,128)S(1)} %pad_maximum_fusion.1), channel_id=1, source_target_pairs={{0,4},{1,5},{2,6},{3,7},{4,0},{5,1},{6,2},{7,3},{8,12},{9,13},{10,... | collective-permute-start | bytes 147464 | tf_op jit(solution)/shard_map/ppermute | solution.py:31
  16.4 2.5 %collective-permute-done.5.refs_6_ = f32[3,32,128]{2,1,0:T(8,128)S(1)} collective-permute-done((f32[3,32,128]{2,1,0:T(8,128)S(1)}, f32[3,32,128]{2,1,0:T(8,128)S(1)}, u32[]{:S(2)}, u32[]{:S(2)}) %collective-permute-start.5) | collective-permute-done | bytes 49184 | tf_op jit(solution)/shard_map/ppermute | solution.py:31
  21.6 2.0 %collective-permute-start.9 = (f32[4,32,128]{2,1,0:T(8,128)S(1)}, f32[4,32,128]{2,1,0:T(8,128)S(1)}, u32[]{:S(2)}, u32[]{:S(2)}) collective-permute-start(f32[4,32,128]{2,1,0:T(8,128)S(1)} %get-tuple-element.78), channel_id=1, source_target_pairs={{0,9},{1,8},{2,11},{3,10},{4,13},{5,12},{6,15},{7,14},{8,17},{9,16... | collective-permute-start | bytes 196616 | tf_op jit(solution)/shard_map/ppermute | solution.py:31
  23.5 1.8 %collective-permute-start.10 = (f32[2,32,128]{2,1,0:T(8,128)S(1)}, f32[2,32,128]{2,1,0:T(8,128)S(1)}, u32[]{:S(2)}, u32[]{:S(2)}) collective-permute-start(f32[2,32,128]{2,1,0:T(8,128)S(1)} %get-tuple-element.83), channel_id=1, source_target_pairs={{0,4},{1,5},{2,6},{3,7},{4,0},{5,1},{6,2},{7,3},{8,12},{9,13},{10,... | collective-permute-start | bytes 98312 | tf_op jit(solution)/shard_map/ppermute | solution.py:31
  26.2 2.2 %collective-permute-start.11 = (f32[3,32,128]{2,1,0:T(8,128)S(1)}, f32[3,32,128]{2,1,0:T(8,128)S(1)}, u32[]{:S(2)}, u32[]{:S(2)}) collective-permute-start(f32[3,32,128]{2,1,0:T(8,128)S(1)} %pad_maximum_fusion.2), channel_id=1, source_target_pairs={{0,6},{1,7},{2,4},{3,5},{4,2},{5,3},{6,0},{7,1},{8,14},{9,15},{10,... | collective-permute-start | bytes 147464 | tf_op jit(solution)/shard_map/ppermute | solution.py:31
  28.6 1.3 %collective-permute-start.13 = (f32[5,32,128]{2,1,0:T(8,128)S(1)}, f32[5,32,128]{2,1,0:T(8,128)S(1)}, u32[]{:S(2)}, u32[]{:S(2)}) collective-permute-start(f32[5,32,128]{2,1,0:T(8,128)S(1)} %constant_dynamic-update-slice_fusion.5), channel_id=1, source_target_pairs={{0,2},{1,3},{2,0},{3,1},{4,6},{5,7},{6,4},{7,5},{8,10},{9,11},{10,... | collective-permute-start | bytes 245768 | tf_op jit(solution)/shard_map/ppermute | solution.py:31
  30.9 1.9 %collective-permute-done.11.refs_5_ = f32[3,32,128]{2,1,0:T(8,128)S(1)} collective-permute-done((f32[3,32,128]{2,1,0:T(8,128)S(1)}, f32[3,32,128]{2,1,0:T(8,128)S(1)}, u32[]{:S(2)}, u32[]{:S(2)}) %collective-permute-start.11) | collective-permute-done | bytes 49184 | tf_op jit(solution)/shard_map/ppermute | solution.py:31
  32.7 2.7 %collective-permute-done.12.refs_6_ = f32[3,32,128]{2,1,0:T(8,128)S(1)} collective-permute-done((f32[3,32,128]{2,1,0:T(8,128)S(1)}, f32[3,32,128]{2,1,0:T(8,128)S(1)}, u32[]{:S(2)}, u32[]{:S(2)}) %collective-permute-start.12) | collective-permute-done | bytes 49184 | tf_op jit(solution)/shard_map/ppermute | solution.py:31
  37.3 1.5 %collective-permute-start.16 = (f32[4,32,128]{2,1,0:T(8,128)S(1)}, f32[4,32,128]{2,1,0:T(8,128)S(1)}, u32[]{:S(2)}, u32[]{:S(2)}) collective-permute-start(f32[4,32,128]{2,1,0:T(8,128)S(1)} %get-tuple-element.87), channel_id=1, source_target_pairs={{0,9},{1,8},{2,11},{3,10},{4,13},{5,12},{6,15},{7,14},{8,17},{9,16... | collective-permute-start | bytes 196616 | tf_op jit(solution)/shard_map/ppermute | solution.py:31
  38.8 1.3 %collective-permute-start.17 = (f32[2,32,128]{2,1,0:T(8,128)S(1)}, f32[2,32,128]{2,1,0:T(8,128)S(1)}, u32[]{:S(2)}, u32[]{:S(2)}) collective-permute-start(f32[2,32,128]{2,1,0:T(8,128)S(1)} %get-tuple-element.92), channel_id=1, source_target_pairs={{0,4},{1,5},{2,6},{3,7},{4,0},{5,1},{6,2},{7,3},{8,12},{9,13},{10,... | collective-permute-start | bytes 98312 | tf_op jit(solution)/shard_map/ppermute | solution.py:31
  40.1 1.1 %collective-permute-done.14.refs_2_ = f32[4,32,128]{2,1,0:T(8,128)S(1)} collective-permute-done((f32[4,32,128]{2,1,0:T(8,128)S(1)}, f32[4,32,128]{2,1,0:T(8,128)S(1)}, u32[]{:S(2)}, u32[]{:S(2)}) %collective-permute-start.14) | collective-permute-done | bytes 65568 | tf_op jit(solution)/shard_map/ppermute | solution.py:31
  41.9 2.1 %collective-permute-start.18 = (f32[3,32,128]{2,1,0:T(8,128)S(1)}, f32[3,32,128]{2,1,0:T(8,128)S(1)}, u32[]{:S(2)}, u32[]{:S(2)}) collective-permute-start(f32[3,32,128]{2,1,0:T(8,128)S(1)} %pad_maximum_fusion.4), channel_id=1, source_target_pairs={{0,6},{1,7},{2,4},{3,5},{4,2},{5,3},{6,0},{7,1},{8,14},{9,15},{10,... | collective-permute-start | bytes 147464 | tf_op jit(solution)/shard_map/ppermute | solution.py:31
  44.5 2.2 %collective-permute-start.19 = (f32[3,32,128]{2,1,0:T(8,128)S(1)}, f32[3,32,128]{2,1,0:T(8,128)S(1)}, u32[]{:S(2)}, u32[]{:S(2)}) collective-permute-start(f32[3,32,128]{2,1,0:T(8,128)S(1)} %pad_maximum_fusion.5), channel_id=1, source_target_pairs={{0,4},{1,5},{2,6},{3,7},{4,0},{5,1},{6,2},{7,3},{8,12},{9,13},{10,... | collective-permute-start | bytes 147464 | tf_op jit(solution)/shard_map/ppermute | solution.py:31
  46.7 1.7 %collective-permute-done.18.refs_5_ = f32[3,32,128]{2,1,0:T(8,128)S(1)} collective-permute-done((f32[3,32,128]{2,1,0:T(8,128)S(1)}, f32[3,32,128]{2,1,0:T(8,128)S(1)}, u32[]{:S(2)}, u32[]{:S(2)}) %collective-permute-start.18) | collective-permute-done | bytes 49184 | tf_op jit(solution)/shard_map/ppermute | solution.py:31
  48.4 1.6 %collective-permute-done.19.refs_6_ = f32[3,32,128]{2,1,0:T(8,128)S(1)} collective-permute-done((f32[3,32,128]{2,1,0:T(8,128)S(1)}, f32[3,32,128]{2,1,0:T(8,128)S(1)}, u32[]{:S(2)}, u32[]{:S(2)}) %collective-permute-start.19) | collective-permute-done | bytes 49184 | tf_op jit(solution)/shard_map/ppermute | solution.py:31
  52.6 1.9 %collective-permute-start.23 = (f32[4,32,128]{2,1,0:T(8,128)S(1)}, f32[4,32,128]{2,1,0:T(8,128)S(1)}, u32[]{:S(2)}, u32[]{:S(2)}) collective-permute-start(f32[4,32,128]{2,1,0:T(8,128)S(1)} %get-tuple-element.96), channel_id=1, source_target_pairs={{0,9},{1,8},{2,11},{3,10},{4,13},{5,12},{6,15},{7,14},{8,17},{9,16... | collective-permute-start | bytes 196616 | tf_op jit(solution)/shard_map/ppermute | solution.py:31
  57.3 1.9 %collective-permute-start.25 = (f32[3,32,128]{2,1,0:T(8,128)S(1)}, f32[3,32,128]{2,1,0:T(8,128)S(1)}, u32[]{:S(2)}, u32[]{:S(2)}) collective-permute-start(f32[3,32,128]{2,1,0:T(8,128)S(1)} %pad_maximum_fusion.6), channel_id=1, source_target_pairs={{0,6},{1,7},{2,4},{3,5},{4,2},{5,3},{6,0},{7,1},{8,14},{9,15},{10,... | collective-permute-start | bytes 147464 | tf_op jit(solution)/shard_map/ppermute | solution.py:31
  60.2 1.9 %collective-permute-start.26 = (f32[3,32,128]{2,1,0:T(8,128)S(1)}, f32[3,32,128]{2,1,0:T(8,128)S(1)}, u32[]{:S(2)}, u32[]{:S(2)}) collective-permute-start(f32[3,32,128]{2,1,0:T(8,128)S(1)} %pad_maximum_fusion.7), channel_id=1, source_target_pairs={{0,4},{1,5},{2,6},{3,7},{4,0},{5,1},{6,2},{7,3},{8,12},{9,13},{10,... | collective-permute-start | bytes 147464 | tf_op jit(solution)/shard_map/ppermute | solution.py:31
  62.2 1.6 %collective-permute-done.25.refs_5_ = f32[3,32,128]{2,1,0:T(8,128)S(1)} collective-permute-done((f32[3,32,128]{2,1,0:T(8,128)S(1)}, f32[3,32,128]{2,1,0:T(8,128)S(1)}, u32[]{:S(2)}, u32[]{:S(2)}) %collective-permute-start.25) | collective-permute-done | bytes 49184 | tf_op jit(solution)/shard_map/ppermute | solution.py:31
  63.8 1.9 %collective-permute-done.26.refs_6_ = f32[3,32,128]{2,1,0:T(8,128)S(1)} collective-permute-done((f32[3,32,128]{2,1,0:T(8,128)S(1)}, f32[3,32,128]{2,1,0:T(8,128)S(1)}, u32[]{:S(2)}, u32[]{:S(2)}) %collective-permute-start.26) | collective-permute-done | bytes 49184 | tf_op jit(solution)/shard_map/ppermute | solution.py:31
  67.0 1.3 %collective-permute-start.28 = (f32[4,32,128]{2,1,0:T(8,128)S(1)}, f32[4,32,128]{2,1,0:T(8,128)S(1)}, u32[]{:S(2)}, u32[]{:S(2)}) collective-permute-start(f32[4,32,128]{2,1,0:T(8,128)S(1)} %get-tuple-element.103), channel_id=1, source_target_pairs={{0,1},{1,0},{2,3},{3,2},{4,5},{5,4},{6,7},{7,6},{8,9},{9,8},{10,11... | collective-permute-start | bytes 196616 | tf_op jit(solution)/shard_map/ppermute | solution.py:31
  68.3 1.4 %collective-permute-start.30 = (f32[4,32,128]{2,1,0:T(8,128)S(1)}, f32[4,32,128]{2,1,0:T(8,128)S(1)}, u32[]{:S(2)}, u32[]{:S(2)}) collective-permute-start(f32[4,32,128]{2,1,0:T(8,128)S(1)} %get-tuple-element.105), channel_id=1, source_target_pairs={{0,9},{1,8},{2,11},{3,10},{4,13},{5,12},{6,15},{7,14},{8,17},{9,16... | collective-permute-start | bytes 196616 | tf_op jit(solution)/shard_map/ppermute | solution.py:31
  73.0 1.7 %collective-permute-start.32 = (f32[3,32,128]{2,1,0:T(8,128)S(1)}, f32[3,32,128]{2,1,0:T(8,128)S(1)}, u32[]{:S(2)}, u32[]{:S(2)}) collective-permute-start(f32[3,32,128]{2,1,0:T(8,128)S(1)} %pad_maximum_fusion.8), channel_id=1, source_target_pairs={{0,6},{1,7},{2,4},{3,5},{4,2},{5,3},{6,0},{7,1},{8,14},{9,15},{10,... | collective-permute-start | bytes 147464 | tf_op jit(solution)/shard_map/ppermute | solution.py:31
  75.4 2.1 %collective-permute-start.33 = (f32[3,32,128]{2,1,0:T(8,128)S(1)}, f32[3,32,128]{2,1,0:T(8,128)S(1)}, u32[]{:S(2)}, u32[]{:S(2)}) collective-permute-start(f32[3,32,128]{2,1,0:T(8,128)S(1)} %pad_maximum_fusion.9), channel_id=1, source_target_pairs={{0,4},{1,5},{2,6},{3,7},{4,0},{5,1},{6,2},{7,3},{8,12},{9,13},{10,... | collective-permute-start | bytes 147464 | tf_op jit(solution)/shard_map/ppermute | solution.py:31
  77.5 1.9 %collective-permute-done.32.refs_5_ = f32[3,32,128]{2,1,0:T(8,128)S(1)} collective-permute-done((f32[3,32,128]{2,1,0:T(8,128)S(1)}, f32[3,32,128]{2,1,0:T(8,128)S(1)}, u32[]{:S(2)}, u32[]{:S(2)}) %collective-permute-start.32) | collective-permute-done | bytes 49184 | tf_op jit(solution)/shard_map/ppermute | solution.py:31
  79.4 1.3 %collective-permute-done.33.refs_6_ = f32[3,32,128]{2,1,0:T(8,128)S(1)} collective-permute-done((f32[3,32,128]{2,1,0:T(8,128)S(1)}, f32[3,32,128]{2,1,0:T(8,128)S(1)}, u32[]{:S(2)}, u32[]{:S(2)}) %collective-permute-start.33) | collective-permute-done | bytes 49184 | tf_op jit(solution)/shard_map/ppermute | solution.py:31
  81.1 2.0 %later_level.9 = (f32[129,32,128]{2,1,0:T(8,128)S(1)}, f32[48,32,128]{2,1,0:T(8,128)}) custom-call(s32[294]{0:T(512)S(1)} %get-tuple-element.59.plan, s32[5,1,8]{2,1,0:T(1,128)S(1)} %get-tuple-element.60.peers, s32[5,1,8]{2,1,0:T(1,128)S(1)} %get-tuple-element.61.downs, s32[4,48]{1,0:T(4,128)S(1)} %get-tuple-element.62.slots, ...), custom_call_target="tpu_custom_call", output_to_operand_aliasing={{0}: (16, {})} | custom-call | tf_op jit(solution)/shard_map/later_level/pallas_call | solution.py:224
  (79 shorter events, 19.9 us)
Async XLA Ops:
  2.3 7.4 %collective-permute-start = (f32[4,32,128]{2,1,0:T(8,128)S(1)}, f32[4,32,128]{2,1,0:T(8,128)S(1)}, u32[]{:S(2)}, u32[]{:S(2)}) collective-permute-start(f32[4,32,128]{2,1,0:T(8,128)S(1)} %get-tuple-element.67), channel_id=1, source_target_pairs={{0,1},{1,0},{2,3},{3,2},{4,5},{5,4},{6,7},{7,6},{8,9},{9,8},{10,11... | collective-permute-start | bytes 196616 | tf_op jit(solution)/shard_map/ppermute | solution.py:31
  5.3 4.4 %collective-permute-start.1 = (f32[4,32,128]{2,1,0:T(8,128)S(1)}, f32[4,32,128]{2,1,0:T(8,128)S(1)}, u32[]{:S(2)}, u32[]{:S(2)}) collective-permute-start(f32[4,32,128]{2,1,0:T(8,128)S(1)} %get-tuple-element.68), channel_id=1, source_target_pairs={{0,8},{1,9},{2,10},{3,11},{4,12},{5,13},{6,14},{7,15},{8,16},{9,17... | collective-permute-start | bytes 196616 | tf_op jit(solution)/shard_map/ppermute | solution.py:31
  5.3 4.6 %collective-permute-start.2 = (f32[4,32,128]{2,1,0:T(8,128)S(1)}, f32[4,32,128]{2,1,0:T(8,128)S(1)}, u32[]{:S(2)}, u32[]{:S(2)}) collective-permute-start(f32[4,32,128]{2,1,0:T(8,128)S(1)} %get-tuple-element.69), channel_id=1, source_target_pairs={{0,9},{1,8},{2,11},{3,10},{4,13},{5,12},{6,15},{7,14},{8,17},{9,16... | collective-permute-start | bytes 196616 | tf_op jit(solution)/shard_map/ppermute | solution.py:31
  7.0 6.5 %collective-permute-start.3 = (f32[2,32,128]{2,1,0:T(8,128)S(1)}, f32[2,32,128]{2,1,0:T(8,128)S(1)}, u32[]{:S(2)}, u32[]{:S(2)}) collective-permute-start(f32[2,32,128]{2,1,0:T(8,128)S(1)} %get-tuple-element.74), channel_id=1, source_target_pairs={{0,4},{1,5},{2,6},{3,7},{4,0},{5,1},{6,2},{7,3},{8,12},{9,13},{10,... | collective-permute-start | bytes 98312 | tf_op jit(solution)/shard_map/ppermute | solution.py:31
  9.9 6.5 %collective-permute-start.4 = (f32[3,32,128]{2,1,0:T(8,128)S(1)}, f32[3,32,128]{2,1,0:T(8,128)S(1)}, u32[]{:S(2)}, u32[]{:S(2)}) collective-permute-start(f32[3,32,128]{2,1,0:T(8,128)S(1)} %pad_maximum_fusion), channel_id=1, source_target_pairs={{0,6},{1,7},{2,4},{3,5},{4,2},{5,3},{6,0},{7,1},{8,14},{9,15},{10,... | collective-permute-start | bytes 147464 | tf_op jit(solution)/shard_map/ppermute | solution.py:31
  13.6 5.9 %collective-permute-start.6 = (f32[5,32,128]{2,1,0:T(8,128)S(1)}, f32[5,32,128]{2,1,0:T(8,128)S(1)}, u32[]{:S(2)}, u32[]{:S(2)}) collective-permute-start(f32[5,32,128]{2,1,0:T(8,128)S(1)} %constant_dynamic-update-slice_fusion), channel_id=1, source_target_pairs={{0,2},{1,3},{2,0},{3,1},{4,6},{5,7},{6,4},{7,5},{8,10},{9,11},{10,... | collective-permute-start | bytes 245768 | tf_op jit(solution)/shard_map/ppermute | solution.py:31
  13.7 5.2 %collective-permute-start.5 = (f32[3,32,128]{2,1,0:T(8,128)S(1)}, f32[3,32,128]{2,1,0:T(8,128)S(1)}, u32[]{:S(2)}, u32[]{:S(2)}) collective-permute-start(f32[3,32,128]{2,1,0:T(8,128)S(1)} %pad_maximum_fusion.1), channel_id=1, source_target_pairs={{0,4},{1,5},{2,6},{3,7},{4,0},{5,1},{6,2},{7,3},{8,12},{9,13},{10,... | collective-permute-start | bytes 147464 | tf_op jit(solution)/shard_map/ppermute | solution.py:31
  20.6 4.8 %collective-permute-start.7 = (f32[4,32,128]{2,1,0:T(8,128)S(1)}, f32[4,32,128]{2,1,0:T(8,128)S(1)}, u32[]{:S(2)}, u32[]{:S(2)}) collective-permute-start(f32[4,32,128]{2,1,0:T(8,128)S(1)} %get-tuple-element.76), channel_id=1, source_target_pairs={{0,1},{1,0},{2,3},{3,2},{4,5},{5,4},{6,7},{7,6},{8,9},{9,8},{10,11... | collective-permute-start | bytes 196616 | tf_op jit(solution)/shard_map/ppermute | solution.py:31
  21.6 4.6 %collective-permute-start.9 = (f32[4,32,128]{2,1,0:T(8,128)S(1)}, f32[4,32,128]{2,1,0:T(8,128)S(1)}, u32[]{:S(2)}, u32[]{:S(2)}) collective-permute-start(f32[4,32,128]{2,1,0:T(8,128)S(1)} %get-tuple-element.78), channel_id=1, source_target_pairs={{0,9},{1,8},{2,11},{3,10},{4,13},{5,12},{6,15},{7,14},{8,17},{9,16... | collective-permute-start | bytes 196616 | tf_op jit(solution)/shard_map/ppermute | solution.py:31
  23.5 5.0 %collective-permute-start.10 = (f32[2,32,128]{2,1,0:T(8,128)S(1)}, f32[2,32,128]{2,1,0:T(8,128)S(1)}, u32[]{:S(2)}, u32[]{:S(2)}) collective-permute-start(f32[2,32,128]{2,1,0:T(8,128)S(1)} %get-tuple-element.83), channel_id=1, source_target_pairs={{0,4},{1,5},{2,6},{3,7},{4,0},{5,1},{6,2},{7,3},{8,12},{9,13},{10,... | collective-permute-start | bytes 98312 | tf_op jit(solution)/shard_map/ppermute | solution.py:31
  26.2 6.5 %collective-permute-start.11 = (f32[3,32,128]{2,1,0:T(8,128)S(1)}, f32[3,32,128]{2,1,0:T(8,128)S(1)}, u32[]{:S(2)}, u32[]{:S(2)}) collective-permute-start(f32[3,32,128]{2,1,0:T(8,128)S(1)} %pad_maximum_fusion.2), channel_id=1, source_target_pairs={{0,6},{1,7},{2,4},{3,5},{4,2},{5,3},{6,0},{7,1},{8,14},{9,15},{10,... | collective-permute-start | bytes 147464 | tf_op jit(solution)/shard_map/ppermute | solution.py:31
  28.6 6.9 %collective-permute-start.13 = (f32[5,32,128]{2,1,0:T(8,128)S(1)}, f32[5,32,128]{2,1,0:T(8,128)S(1)}, u32[]{:S(2)}, u32[]{:S(2)}) collective-permute-start(f32[5,32,128]{2,1,0:T(8,128)S(1)} %constant_dynamic-update-slice_fusion.5), channel_id=1, source_target_pairs={{0,2},{1,3},{2,0},{3,1},{4,6},{5,7},{6,4},{7,5},{8,10},{9,11},{10,... | collective-permute-start | bytes 245768 | tf_op jit(solution)/shard_map/ppermute | solution.py:31
  29.9 5.5 %collective-permute-start.12 = (f32[3,32,128]{2,1,0:T(8,128)S(1)}, f32[3,32,128]{2,1,0:T(8,128)S(1)}, u32[]{:S(2)}, u32[]{:S(2)}) collective-permute-start(f32[3,32,128]{2,1,0:T(8,128)S(1)} %pad_maximum_fusion.3), channel_id=1, source_target_pairs={{0,4},{1,5},{2,6},{3,7},{4,0},{5,1},{6,2},{7,3},{8,12},{9,13},{10,... | collective-permute-start | bytes 147464 | tf_op jit(solution)/shard_map/ppermute | solution.py:31
  36.5 4.7 %collective-permute-start.14 = (f32[4,32,128]{2,1,0:T(8,128)S(1)}, f32[4,32,128]{2,1,0:T(8,128)S(1)}, u32[]{:S(2)}, u32[]{:S(2)}) collective-permute-start(f32[4,32,128]{2,1,0:T(8,128)S(1)} %get-tuple-element.85), channel_id=1, source_target_pairs={{0,1},{1,0},{2,3},{3,2},{4,5},{5,4},{6,7},{7,6},{8,9},{9,8},{10,11... | collective-permute-start | bytes 196616 | tf_op jit(solution)/shard_map/ppermute | solution.py:31
  37.3 3.9 %collective-permute-start.15 = (f32[4,32,128]{2,1,0:T(8,128)S(1)}, f32[4,32,128]{2,1,0:T(8,128)S(1)}, u32[]{:S(2)}, u32[]{:S(2)}) collective-permute-start(f32[4,32,128]{2,1,0:T(8,128)S(1)} %get-tuple-element.86), channel_id=1, source_target_pairs={{0,8},{1,9},{2,10},{3,11},{4,12},{5,13},{6,14},{7,15},{8,16},{9,17... | collective-permute-start | bytes 196616 | tf_op jit(solution)/shard_map/ppermute | solution.py:31
  37.3 4.6 %collective-permute-start.16 = (f32[4,32,128]{2,1,0:T(8,128)S(1)}, f32[4,32,128]{2,1,0:T(8,128)S(1)}, u32[]{:S(2)}, u32[]{:S(2)}) collective-permute-start(f32[4,32,128]{2,1,0:T(8,128)S(1)} %get-tuple-element.87), channel_id=1, source_target_pairs={{0,9},{1,8},{2,11},{3,10},{4,13},{5,12},{6,15},{7,14},{8,17},{9,16... | collective-permute-start | bytes 196616 | tf_op jit(solution)/shard_map/ppermute | solution.py:31
  38.8 5.3 %collective-permute-start.17 = (f32[2,32,128]{2,1,0:T(8,128)S(1)}, f32[2,32,128]{2,1,0:T(8,128)S(1)}, u32[]{:S(2)}, u32[]{:S(2)}) collective-permute-start(f32[2,32,128]{2,1,0:T(8,128)S(1)} %get-tuple-element.92), channel_id=1, source_target_pairs={{0,4},{1,5},{2,6},{3,7},{4,0},{5,1},{6,2},{7,3},{8,12},{9,13},{10,... | collective-permute-start | bytes 98312 | tf_op jit(solution)/shard_map/ppermute | solution.py:31
  41.9 6.5 %collective-permute-start.18 = (f32[3,32,128]{2,1,0:T(8,128)S(1)}, f32[3,32,128]{2,1,0:T(8,128)S(1)}, u32[]{:S(2)}, u32[]{:S(2)}) collective-permute-start(f32[3,32,128]{2,1,0:T(8,128)S(1)} %pad_maximum_fusion.4), channel_id=1, source_target_pairs={{0,6},{1,7},{2,4},{3,5},{4,2},{5,3},{6,0},{7,1},{8,14},{9,15},{10,... | collective-permute-start | bytes 147464 | tf_op jit(solution)/shard_map/ppermute | solution.py:31
  44.1 6.4 %collective-permute-start.20 = (f32[5,32,128]{2,1,0:T(8,128)S(1)}, f32[5,32,128]{2,1,0:T(8,128)S(1)}, u32[]{:S(2)}, u32[]{:S(2)}) collective-permute-start(f32[5,32,128]{2,1,0:T(8,128)S(1)} %constant_dynamic-update-slice_fusion.10), channel_id=1, source_target_pairs={{0,2},{1,3},{2,0},{3,1},{4,6},{5,7},{6,4},{7,5},{8,10},{9,11},{10,... | collective-permute-start | bytes 245768 | tf_op jit(solution)/shard_map/ppermute | solution.py:31
  44.5 5.5 %collective-permute-start.19 = (f32[3,32,128]{2,1,0:T(8,128)S(1)}, f32[3,32,128]{2,1,0:T(8,128)S(1)}, u32[]{:S(2)}, u32[]{:S(2)}) collective-permute-start(f32[3,32,128]{2,1,0:T(8,128)S(1)} %pad_maximum_fusion.5), channel_id=1, source_target_pairs={{0,4},{1,5},{2,6},{3,7},{4,0},{5,1},{6,2},{7,3},{8,12},{9,13},{10,... | collective-permute-start | bytes 147464 | tf_op jit(solution)/shard_map/ppermute | solution.py:31
  51.5 4.3 %collective-permute-start.21 = (f32[4,32,128]{2,1,0:T(8,128)S(1)}, f32[4,32,128]{2,1,0:T(8,128)S(1)}, u32[]{:S(2)}, u32[]{:S(2)}) collective-permute-start(f32[4,32,128]{2,1,0:T(8,128)S(1)} %get-tuple-element.94), channel_id=1, source_target_pairs={{0,1},{1,0},{2,3},{3,2},{4,5},{5,4},{6,7},{7,6},{8,9},{9,8},{10,11... | collective-permute-start | bytes 196616 | tf_op jit(solution)/shard_map/ppermute | solution.py:31
  52.6 4.6 %collective-permute-start.23 = (f32[4,32,128]{2,1,0:T(8,128)S(1)}, f32[4,32,128]{2,1,0:T(8,128)S(1)}, u32[]{:S(2)}, u32[]{:S(2)}) collective-permute-start(f32[4,32,128]{2,1,0:T(8,128)S(1)} %get-tuple-element.96), channel_id=1, source_target_pairs={{0,9},{1,8},{2,11},{3,10},{4,13},{5,12},{6,15},{7,14},{8,17},{9,16... | collective-permute-start | bytes 196616 | tf_op jit(solution)/shard_map/ppermute | solution.py:31
  54.6 5.2 %collective-permute-start.24 = (f32[2,32,128]{2,1,0:T(8,128)S(1)}, f32[2,32,128]{2,1,0:T(8,128)S(1)}, u32[]{:S(2)}, u32[]{:S(2)}) collective-permute-start(f32[2,32,128]{2,1,0:T(8,128)S(1)} %get-tuple-element.101), channel_id=1, source_target_pairs={{0,4},{1,5},{2,6},{3,7},{4,0},{5,1},{6,2},{7,3},{8,12},{9,13},{10,... | collective-permute-start | bytes 98312 | tf_op jit(solution)/shard_map/ppermute | solution.py:31
  57.3 6.5 %collective-permute-start.25 = (f32[3,32,128]{2,1,0:T(8,128)S(1)}, f32[3,32,128]{2,1,0:T(8,128)S(1)}, u32[]{:S(2)}, u32[]{:S(2)}) collective-permute-start(f32[3,32,128]{2,1,0:T(8,128)S(1)} %pad_maximum_fusion.6), channel_id=1, source_target_pairs={{0,6},{1,7},{2,4},{3,5},{4,2},{5,3},{6,0},{7,1},{8,14},{9,15},{10,... | collective-permute-start | bytes 147464 | tf_op jit(solution)/shard_map/ppermute | solution.py:31
  59.8 6.2 %collective-permute-start.27 = (f32[5,32,128]{2,1,0:T(8,128)S(1)}, f32[5,32,128]{2,1,0:T(8,128)S(1)}, u32[]{:S(2)}, u32[]{:S(2)}) collective-permute-start(f32[5,32,128]{2,1,0:T(8,128)S(1)} %constant_dynamic-update-slice_fusion.15), channel_id=1, source_target_pairs={{0,2},{1,3},{2,0},{3,1},{4,6},{5,7},{6,4},{7,5},{8,10},{9,11},{10,... | collective-permute-start | bytes 245768 | tf_op jit(solution)/shard_map/ppermute | solution.py:31
  60.2 5.4 %collective-permute-start.26 = (f32[3,32,128]{2,1,0:T(8,128)S(1)}, f32[3,32,128]{2,1,0:T(8,128)S(1)}, u32[]{:S(2)}, u32[]{:S(2)}) collective-permute-start(f32[3,32,128]{2,1,0:T(8,128)S(1)} %pad_maximum_fusion.7), channel_id=1, source_target_pairs={{0,4},{1,5},{2,6},{3,7},{4,0},{5,1},{6,2},{7,3},{8,12},{9,13},{10,... | collective-permute-start | bytes 147464 | tf_op jit(solution)/shard_map/ppermute | solution.py:31
  67.0 4.3 %collective-permute-start.28 = (f32[4,32,128]{2,1,0:T(8,128)S(1)}, f32[4,32,128]{2,1,0:T(8,128)S(1)}, u32[]{:S(2)}, u32[]{:S(2)}) collective-permute-start(f32[4,32,128]{2,1,0:T(8,128)S(1)} %get-tuple-element.103), channel_id=1, source_target_pairs={{0,1},{1,0},{2,3},{3,2},{4,5},{5,4},{6,7},{7,6},{8,9},{9,8},{10,11... | collective-permute-start | bytes 196616 | tf_op jit(solution)/shard_map/ppermute | solution.py:31
  68.3 4.6 %collective-permute-start.30 = (f32[4,32,128]{2,1,0:T(8,128)S(1)}, f32[4,32,128]{2,1,0:T(8,128)S(1)}, u32[]{:S(2)}, u32[]{:S(2)}) collective-permute-start(f32[4,32,128]{2,1,0:T(8,128)S(1)} %get-tuple-element.105), channel_id=1, source_target_pairs={{0,9},{1,8},{2,11},{3,10},{4,13},{5,12},{6,15},{7,14},{8,17},{9,16... | collective-permute-start | bytes 196616 | tf_op jit(solution)/shard_map/ppermute | solution.py:31
  69.7 5.2 %collective-permute-start.31 = (f32[2,32,128]{2,1,0:T(8,128)S(1)}, f32[2,32,128]{2,1,0:T(8,128)S(1)}, u32[]{:S(2)}, u32[]{:S(2)}) collective-permute-start(f32[2,32,128]{2,1,0:T(8,128)S(1)} %get-tuple-element.110), channel_id=1, source_target_pairs={{0,4},{1,5},{2,6},{3,7},{4,0},{5,1},{6,2},{7,3},{8,12},{9,13},{10,... | collective-permute-start | bytes 98312 | tf_op jit(solution)/shard_map/ppermute | solution.py:31
  73.0 6.5 %collective-permute-start.32 = (f32[3,32,128]{2,1,0:T(8,128)S(1)}, f32[3,32,128]{2,1,0:T(8,128)S(1)}, u32[]{:S(2)}, u32[]{:S(2)}) collective-permute-start(f32[3,32,128]{2,1,0:T(8,128)S(1)} %pad_maximum_fusion.8), channel_id=1, source_target_pairs={{0,6},{1,7},{2,4},{3,5},{4,2},{5,3},{6,0},{7,1},{8,14},{9,15},{10,... | collective-permute-start | bytes 147464 | tf_op jit(solution)/shard_map/ppermute | solution.py:31
  74.9 6.2 %collective-permute-start.34 = (f32[5,32,128]{2,1,0:T(8,128)S(1)}, f32[5,32,128]{2,1,0:T(8,128)S(1)}, u32[]{:S(2)}, u32[]{:S(2)}) collective-permute-start(f32[5,32,128]{2,1,0:T(8,128)S(1)} %constant_dynamic-update-slice_fusion.20), channel_id=1, source_target_pairs={{0,2},{1,3},{2,0},{3,1},{4,6},{5,7},{6,4},{7,5},{8,10},{9,11},{10,... | collective-permute-start | bytes 245768 | tf_op jit(solution)/shard_map/ppermute | solution.py:31
  75.4 5.4 %collective-permute-start.33 = (f32[3,32,128]{2,1,0:T(8,128)S(1)}, f32[3,32,128]{2,1,0:T(8,128)S(1)}, u32[]{:S(2)}, u32[]{:S(2)}) collective-permute-start(f32[3,32,128]{2,1,0:T(8,128)S(1)} %pad_maximum_fusion.9), channel_id=1, source_target_pairs={{0,4},{1,5},{2,6},{3,7},{4,0},{5,1},{6,2},{7,3},{8,12},{9,13},{10,... | collective-permute-start | bytes 147464 | tf_op jit(solution)/shard_map/ppermute | solution.py:31
  (3 other events, 11.2 us)
where the time goes:
time: 83.2 us; the launch traced here: 83.1 us
  starting transfers between devices  48 us (58%)
  waiting for transfers between devices  26.1 us (31%)
  Pallas kernels  8.55 us (10%)
    ppermute x35, starting transfers between devices, moved(): return lax.ppermute(value, ('section', 'blk'), pairs)  48 us
    ppermute x35, waiting for transfers between devices, moved(): return lax.ppermute(value, ('section', 'blk'), pairs)  26.1 us
    pallas_call x5, Pallas kernels, shards(): pl.pallas_call(functools.partial(later_level, level, rows, columns), in_s...  6.3 us
    pallas_call x1, Pallas kernels, shards(): pl.pallas_call(functools.partial(first_level, rows, columns), in_specs=[h...  2.25 us
  transfers between devices with their start and end apart: 35, of which 27 were waited for; matrix products, arithmetic and copies ran while one was open for 0% of the time, Pallas kernels for 0%

commit v1 on v0

--- a/solution.py
+++ b/solution.py
@@ -33,6 +33,11 @@
 
 def halves_of(rows):
     return rows // 2 if rows > 1 and rows & (rows - 1) == 0 else rows
+
+
+def row_steps(rows):
+    half = halves_of(rows)
+    return list(range(half, rows)) + list(range(1, half))
 
 
 def wrapped(value, count):
@@ -125,7 +130,7 @@
     from_above = [refs.pop(0) for _ in range(columns)]
     over_columns = [None] + [refs.pop(0) for _ in range(1, columns)]
     own_column = [refs.pop(0) for _ in range(rows // half)]
-    arrived = {step: refs.pop(0) for step in range(rows - 1, 0, -1)}
+    arrived = {step: refs.pop(0) for step in row_steps(rows)}
     refs.pop(0)
     pool = refs.pop(0)
     outs = refs
@@ -211,7 +216,7 @@
         if half < rows:
             own_column[1] = moved(own_column[1], sections, rows, columns, (0, half, 0))
         arrived = []
-        for step in range(rows - 1, 0, -1):
+        for step in row_steps(rows):
             part = [value[step] for value in over_columns + from_above]
             if step < half:
                 part += [value[step] for value in own_column]

time: 83.2 us -> 83.6 us (level)
  waiting for transfers between devices: 26.1 us -> 35.2 us
  starting transfers between devices: 48 us -> 39.4 us
    ppermute x35, waiting for transfers between devices: 26.1 us -> 35.2 us  [moved(): return lax.ppermute(value, ('section', 'blk'), pairs)]
    ppermute x35, starting transfers between devices: 48 us -> 39.4 us  [moved(): return lax.ppermute(value, ('section', 'blk'), pairs)]
  transfers between devices with their start and end apart: 35 -> 35, of which waited for: 27 -> 26; matrix products, arithmetic and copies ran while one was open for 0% -> 0% of each run, Pallas kernels for 0% -> 0%
where the time goes in v1:
time: 83.6 us; the launch traced here: 83.5 us
  starting transfers between devices  39.4 us (47%)
  waiting for transfers between devices  35.2 us (42%)
  Pallas kernels  8.55 us (10%)
    ppermute x35, starting transfers between devices, moved(): return lax.ppermute(value, ('section', 'blk'), pairs)  39.4 us
    ppermute x35, waiting for transfers between devices, moved(): return lax.ppermute(value, ('section', 'blk'), pairs)  35.2 us
    pallas_call x5, Pallas kernels, shards(): pl.pallas_call(functools.partial(later_level, level, rows, columns), in_s...  6.3 us
    pallas_call x1, Pallas kernels, shards(): pl.pallas_call(functools.partial(first_level, rows, columns), in_specs=[h...  2.25 us
  transfers between devices with their start and end apart: 35, of which 26 were waited for; matrix products, arithmetic and copies ran while one was open for 0% of the time, Pallas kernels for 0%

profile of v1, /device:TPU:0, one launch (start us, length us, event | category | flops | bytes accessed | tf_op | source)
XLA Modules:
  0.0 83.5 jit_solution(18322610715532320549)
XLA Ops:
  0.0 2.3 %first_level.1 = (f32[129,32,128]{2,1,0:T(8,128)S(1)}, f32[48,32,32]{2,1,0:T(8,128)S(1)}, s32[294]{0:T(512)S(1)}, s32[5,1,8]{2,1,0:T(1,128)S(1)}, s32[5,1,8]{2,1...) custom-call(s32[48]{0:T(128)} %refs_0_.1, ...), custom_call_target="tpu_custom_call" | custom-call | tf_op jit(solution)/shard_map/first_level/pallas_call | solution.py:194
  2.3 3.0 %collective-permute-start = (f32[4,32,128]{2,1,0:T(8,128)S(1)}, f32[4,32,128]{2,1,0:T(8,128)S(1)}, u32[]{:S(2)}, u32[]{:S(2)}) collective-permute-start(f32[4,32,128]{2,1,0:T(8,128)S(1)} %get-tuple-element.67), channel_id=1, source_target_pairs={{0,1},{1,0},{2,3},{3,2},{4,5},{5,4},{6,7},{7,6},{8,9},{9,8},{10,11... | collective-permute-start | bytes 196616 | tf_op jit(solution)/shard_map/ppermute | solution.py:31
  5.3 1.8 %collective-permute-start.2 = (f32[4,32,128]{2,1,0:T(8,128)S(1)}, f32[4,32,128]{2,1,0:T(8,128)S(1)}, u32[]{:S(2)}, u32[]{:S(2)}) collective-permute-start(f32[4,32,128]{2,1,0:T(8,128)S(1)} %get-tuple-element.69), channel_id=1, source_target_pairs={{0,9},{1,8},{2,11},{3,10},{4,13},{5,12},{6,15},{7,14},{8,17},{9,16... | collective-permute-start | bytes 196616 | tf_op jit(solution)/shard_map/ppermute | solution.py:31
  7.0 2.6 %collective-permute-start.3 = (f32[2,32,128]{2,1,0:T(8,128)S(1)}, f32[2,32,128]{2,1,0:T(8,128)S(1)}, u32[]{:S(2)}, u32[]{:S(2)}) collective-permute-start(f32[2,32,128]{2,1,0:T(8,128)S(1)} %get-tuple-element.74), channel_id=1, source_target_pairs={{0,4},{1,5},{2,6},{3,7},{4,0},{5,1},{6,2},{7,3},{8,12},{9,13},{10,... | collective-permute-start | bytes 98312 | tf_op jit(solution)/shard_map/ppermute | solution.py:31
  9.9 2.7 %collective-permute-start.4 = (f32[3,32,128]{2,1,0:T(8,128)S(1)}, f32[3,32,128]{2,1,0:T(8,128)S(1)}, u32[]{:S(2)}, u32[]{:S(2)}) collective-permute-start(f32[3,32,128]{2,1,0:T(8,128)S(1)} %pad_maximum_fusion), channel_id=1, source_target_pairs={{0,4},{1,5},{2,6},{3,7},{4,0},{5,1},{6,2},{7,3},{8,12},{9,13},{10,... | collective-permute-start | bytes 147464 | tf_op jit(solution)/shard_map/ppermute | solution.py:31
  12.6 1.6 %collective-permute-start.6 = (f32[5,32,128]{2,1,0:T(8,128)S(1)}, f32[5,32,128]{2,1,0:T(8,128)S(1)}, u32[]{:S(2)}, u32[]{:S(2)}) collective-permute-start(f32[5,32,128]{2,1,0:T(8,128)S(1)} %constant_dynamic-update-slice_fusion), channel_id=1, source_target_pairs={{0,2},{1,3},{2,0},{3,1},{4,6},{5,7},{6,4},{7,5},{8,10},{9,11},{10,... | collective-permute-start | bytes 245768 | tf_op jit(solution)/shard_map/ppermute | solution.py:31
  14.2 1.7 %collective-permute-start.5 = (f32[3,32,128]{2,1,0:T(8,128)S(1)}, f32[3,32,128]{2,1,0:T(8,128)S(1)}, u32[]{:S(2)}, u32[]{:S(2)}) collective-permute-start(f32[3,32,128]{2,1,0:T(8,128)S(1)} %pad_maximum_fusion.1), channel_id=1, source_target_pairs={{0,6},{1,7},{2,4},{3,5},{4,2},{5,3},{6,0},{7,1},{8,14},{9,15},{10,... | collective-permute-start | bytes 147464 | tf_op jit(solution)/shard_map/ppermute | solution.py:31
  15.9 4.2 %collective-permute-done.5.refs_6_ = f32[3,32,128]{2,1,0:T(8,128)S(1)} collective-permute-done((f32[3,32,128]{2,1,0:T(8,128)S(1)}, f32[3,32,128]{2,1,0:T(8,128)S(1)}, u32[]{:S(2)}, u32[]{:S(2)}) %collective-permute-start.5) | collective-permute-done | bytes 49184 | tf_op jit(solution)/shard_map/ppermute | solution.py:31
  21.2 1.3 %collective-permute-start.7 = (f32[4,32,128]{2,1,0:T(8,128)S(1)}, f32[4,32,128]{2,1,0:T(8,128)S(1)}, u32[]{:S(2)}, u32[]{:S(2)}) collective-permute-start(f32[4,32,128]{2,1,0:T(8,128)S(1)} %get-tuple-element.76), channel_id=1, source_target_pairs={{0,1},{1,0},{2,3},{3,2},{4,5},{5,4},{6,7},{7,6},{8,9},{9,8},{10,11... | collective-permute-start | bytes 196616 | tf_op jit(solution)/shard_map/ppermute | solution.py:31
  22.5 2.1 %collective-permute-start.9 = (f32[4,32,128]{2,1,0:T(8,128)S(1)}, f32[4,32,128]{2,1,0:T(8,128)S(1)}, u32[]{:S(2)}, u32[]{:S(2)}) collective-permute-start(f32[4,32,128]{2,1,0:T(8,128)S(1)} %get-tuple-element.78), channel_id=1, source_target_pairs={{0,9},{1,8},{2,11},{3,10},{4,13},{5,12},{6,15},{7,14},{8,17},{9,16... | collective-permute-start | bytes 196616 | tf_op jit(solution)/shard_map/ppermute | solution.py:31
  27.7 1.6 %collective-permute-done.10.refs_4_ = f32[2,32,128]{2,1,0:T(8,128)S(1)} collective-permute-done((f32[2,32,128]{2,1,0:T(8,128)S(1)}, f32[2,32,128]{2,1,0:T(8,128)S(1)}, u32[]{:S(2)}, u32[]{:S(2)}) %collective-permute-start.10) | collective-permute-done | bytes 32800 | tf_op jit(solution)/shard_map/ppermute | solution.py:31
  29.8 1.9 %collective-permute-start.12 = (f32[3,32,128]{2,1,0:T(8,128)S(1)}, f32[3,32,128]{2,1,0:T(8,128)S(1)}, u32[]{:S(2)}, u32[]{:S(2)}) collective-permute-start(f32[3,32,128]{2,1,0:T(8,128)S(1)} %pad_maximum_fusion.3), channel_id=1, source_target_pairs={{0,6},{1,7},{2,4},{3,5},{4,2},{5,3},{6,0},{7,1},{8,14},{9,15},{10,... | collective-permute-start | bytes 147464 | tf_op jit(solution)/shard_map/ppermute | solution.py:31
  32.7 3.0 %collective-permute-done.12.refs_6_ = f32[3,32,128]{2,1,0:T(8,128)S(1)} collective-permute-done((f32[3,32,128]{2,1,0:T(8,128)S(1)}, f32[3,32,128]{2,1,0:T(8,128)S(1)}, u32[]{:S(2)}, u32[]{:S(2)}) %collective-permute-start.12) | collective-permute-done | bytes 49184 | tf_op jit(solution)/shard_map/ppermute | solution.py:31
  37.6 1.6 %collective-permute-start.16 = (f32[4,32,128]{2,1,0:T(8,128)S(1)}, f32[4,32,128]{2,1,0:T(8,128)S(1)}, u32[]{:S(2)}, u32[]{:S(2)}) collective-permute-start(f32[4,32,128]{2,1,0:T(8,128)S(1)} %get-tuple-element.87), channel_id=1, source_target_pairs={{0,9},{1,8},{2,11},{3,10},{4,13},{5,12},{6,15},{7,14},{8,17},{9,16... | collective-permute-start | bytes 196616 | tf_op jit(solution)/shard_map/ppermute | solution.py:31
  39.2 1.2 %collective-permute-start.17 = (f32[2,32,128]{2,1,0:T(8,128)S(1)}, f32[2,32,128]{2,1,0:T(8,128)S(1)}, u32[]{:S(2)}, u32[]{:S(2)}) collective-permute-start(f32[2,32,128]{2,1,0:T(8,128)S(1)} %get-tuple-element.92), channel_id=1, source_target_pairs={{0,4},{1,5},{2,6},{3,7},{4,0},{5,1},{6,2},{7,3},{8,12},{9,13},{10,... | collective-permute-start | bytes 98312 | tf_op jit(solution)/shard_map/ppermute | solution.py:31
  42.6 1.7 %collective-permute-done.17.refs_4_ = f32[2,32,128]{2,1,0:T(8,128)S(1)} collective-permute-done((f32[2,32,128]{2,1,0:T(8,128)S(1)}, f32[2,32,128]{2,1,0:T(8,128)S(1)}, u32[]{:S(2)}, u32[]{:S(2)}) %collective-permute-start.17) | collective-permute-done | bytes 32800 | tf_op jit(solution)/shard_map/ppermute | solution.py:31
  44.8 1.9 %collective-permute-start.19 = (f32[3,32,128]{2,1,0:T(8,128)S(1)}, f32[3,32,128]{2,1,0:T(8,128)S(1)}, u32[]{:S(2)}, u32[]{:S(2)}) collective-permute-start(f32[3,32,128]{2,1,0:T(8,128)S(1)} %pad_maximum_fusion.5), channel_id=1, source_target_pairs={{0,6},{1,7},{2,4},{3,5},{4,2},{5,3},{6,0},{7,1},{8,14},{9,15},{10,... | collective-permute-start | bytes 147464 | tf_op jit(solution)/shard_map/ppermute | solution.py:31
  46.8 1.5 %collective-permute-done.18.refs_5_ = f32[3,32,128]{2,1,0:T(8,128)S(1)} collective-permute-done((f32[3,32,128]{2,1,0:T(8,128)S(1)}, f32[3,32,128]{2,1,0:T(8,128)S(1)}, u32[]{:S(2)}, u32[]{:S(2)}) %collective-permute-start.18) | collective-permute-done | bytes 49184 | tf_op jit(solution)/shard_map/ppermute | solution.py:31
  48.2 2.5 %collective-permute-done.19.refs_6_ = f32[3,32,128]{2,1,0:T(8,128)S(1)} collective-permute-done((f32[3,32,128]{2,1,0:T(8,128)S(1)}, f32[3,32,128]{2,1,0:T(8,128)S(1)}, u32[]{:S(2)}, u32[]{:S(2)}) %collective-permute-start.19) | collective-permute-done | bytes 49184 | tf_op jit(solution)/shard_map/ppermute | solution.py:31
  51.9 1.3 %collective-permute-start.21 = (f32[4,32,128]{2,1,0:T(8,128)S(1)}, f32[4,32,128]{2,1,0:T(8,128)S(1)}, u32[]{:S(2)}, u32[]{:S(2)}) collective-permute-start(f32[4,32,128]{2,1,0:T(8,128)S(1)} %get-tuple-element.94), channel_id=1, source_target_pairs={{0,1},{1,0},{2,3},{3,2},{4,5},{5,4},{6,7},{7,6},{8,9},{9,8},{10,11... | collective-permute-start | bytes 196616 | tf_op jit(solution)/shard_map/ppermute | solution.py:31
  53.2 1.9 %collective-permute-start.23 = (f32[4,32,128]{2,1,0:T(8,128)S(1)}, f32[4,32,128]{2,1,0:T(8,128)S(1)}, u32[]{:S(2)}, u32[]{:S(2)}) collective-permute-start(f32[4,32,128]{2,1,0:T(8,128)S(1)} %get-tuple-element.96), channel_id=1, source_target_pairs={{0,9},{1,8},{2,11},{3,10},{4,13},{5,12},{6,15},{7,14},{8,17},{9,16... | collective-permute-start | bytes 196616 | tf_op jit(solution)/shard_map/ppermute | solution.py:31
  58.4 1.6 %collective-permute-done.24.refs_4_ = f32[2,32,128]{2,1,0:T(8,128)S(1)} collective-permute-done((f32[2,32,128]{2,1,0:T(8,128)S(1)}, f32[2,32,128]{2,1,0:T(8,128)S(1)}, u32[]{:S(2)}, u32[]{:S(2)}) %collective-permute-start.24) | collective-permute-done | bytes 32800 | tf_op jit(solution)/shard_map/ppermute | solution.py:31
  60.4 1.9 %collective-permute-start.26 = (f32[3,32,128]{2,1,0:T(8,128)S(1)}, f32[3,32,128]{2,1,0:T(8,128)S(1)}, u32[]{:S(2)}, u32[]{:S(2)}) collective-permute-start(f32[3,32,128]{2,1,0:T(8,128)S(1)} %pad_maximum_fusion.7), channel_id=1, source_target_pairs={{0,6},{1,7},{2,4},{3,5},{4,2},{5,3},{6,0},{7,1},{8,14},{9,15},{10,... | collective-permute-start | bytes 147464 | tf_op jit(solution)/shard_map/ppermute | solution.py:31
  62.4 1.1 %collective-permute-done.25.refs_5_ = f32[3,32,128]{2,1,0:T(8,128)S(1)} collective-permute-done((f32[3,32,128]{2,1,0:T(8,128)S(1)}, f32[3,32,128]{2,1,0:T(8,128)S(1)}, u32[]{:S(2)}, u32[]{:S(2)}) %collective-permute-start.25) | collective-permute-done | bytes 49184 | tf_op jit(solution)/shard_map/ppermute | solution.py:31
  63.5 2.8 %collective-permute-done.26.refs_6_ = f32[3,32,128]{2,1,0:T(8,128)S(1)} collective-permute-done((f32[3,32,128]{2,1,0:T(8,128)S(1)}, f32[3,32,128]{2,1,0:T(8,128)S(1)}, u32[]{:S(2)}, u32[]{:S(2)}) %collective-permute-start.26) | collective-permute-done | bytes 49184 | tf_op jit(solution)/shard_map/ppermute | solution.py:31
  68.3 1.8 %collective-permute-start.30 = (f32[4,32,128]{2,1,0:T(8,128)S(1)}, f32[4,32,128]{2,1,0:T(8,128)S(1)}, u32[]{:S(2)}, u32[]{:S(2)}) collective-permute-start(f32[4,32,128]{2,1,0:T(8,128)S(1)} %get-tuple-element.105), channel_id=1, source_target_pairs={{0,9},{1,8},{2,11},{3,10},{4,13},{5,12},{6,15},{7,14},{8,17},{9,16... | collective-permute-start | bytes 196616 | tf_op jit(solution)/shard_map/ppermute | solution.py:31
  70.7 1.1 %collective-permute-done.28.refs_2_ = f32[4,32,128]{2,1,0:T(8,128)S(1)} collective-permute-done((f32[4,32,128]{2,1,0:T(8,128)S(1)}, f32[4,32,128]{2,1,0:T(8,128)S(1)}, u32[]{:S(2)}, u32[]{:S(2)}) %collective-permute-start.28) | collective-permute-done | bytes 65568 | tf_op jit(solution)/shard_map/ppermute | solution.py:31
  73.0 1.3 %collective-permute-start.32 = (f32[3,32,128]{2,1,0:T(8,128)S(1)}, f32[3,32,128]{2,1,0:T(8,128)S(1)}, u32[]{:S(2)}, u32[]{:S(2)}) collective-permute-start(f32[3,32,128]{2,1,0:T(8,128)S(1)} %pad_maximum_fusion.8), channel_id=1, source_target_pairs={{0,4},{1,5},{2,6},{3,7},{4,0},{5,1},{6,2},{7,3},{8,12},{9,13},{10,... | collective-permute-start | bytes 147464 | tf_op jit(solution)/shard_map/ppermute | solution.py:31
  75.6 1.9 %collective-permute-start.33 = (f32[3,32,128]{2,1,0:T(8,128)S(1)}, f32[3,32,128]{2,1,0:T(8,128)S(1)}, u32[]{:S(2)}, u32[]{:S(2)}) collective-permute-start(f32[3,32,128]{2,1,0:T(8,128)S(1)} %pad_maximum_fusion.9), channel_id=1, source_target_pairs={{0,6},{1,7},{2,4},{3,5},{4,2},{5,3},{6,0},{7,1},{8,14},{9,15},{10,... | collective-permute-start | bytes 147464 | tf_op jit(solution)/shard_map/ppermute | solution.py:31
  77.5 1.4 %collective-permute-done.32.refs_5_ = f32[3,32,128]{2,1,0:T(8,128)S(1)} collective-permute-done((f32[3,32,128]{2,1,0:T(8,128)S(1)}, f32[3,32,128]{2,1,0:T(8,128)S(1)}, u32[]{:S(2)}, u32[]{:S(2)}) %collective-permute-start.32) | collective-permute-done | bytes 49184 | tf_op jit(solution)/shard_map/ppermute | solution.py:31
  78.9 2.6 %collective-permute-done.33.refs_6_ = f32[3,32,128]{2,1,0:T(8,128)S(1)} collective-permute-done((f32[3,32,128]{2,1,0:T(8,128)S(1)}, f32[3,32,128]{2,1,0:T(8,128)S(1)}, u32[]{:S(2)}, u32[]{:S(2)}) %collective-permute-start.33) | collective-permute-done | bytes 49184 | tf_op jit(solution)/shard_map/ppermute | solution.py:31
  81.5 2.0 %later_level.9 = (f32[129,32,128]{2,1,0:T(8,128)S(1)}, f32[48,32,128]{2,1,0:T(8,128)}) custom-call(s32[294]{0:T(512)S(1)} %get-tuple-element.59.plan, s32[5,1,8]{2,1,0:T(1,128)S(1)} %get-tuple-element.60.peers, s32[5,1,8]{2,1,0:T(1,128)S(1)} %get-tuple-element.61.downs, s32[4,48]{1,0:T(4,128)S(1)} %get-tuple-element.62.slots, ...), custom_call_target="tpu_custom_call", output_to_operand_aliasing={{0}: (16, {})} | custom-call | tf_op jit(solution)/shard_map/later_level/pallas_call | solution.py:229
  (79 shorter events, 20.3 us)
Async XLA Ops:
  2.3 7.4 %collective-permute-start = (f32[4,32,128]{2,1,0:T(8,128)S(1)}, f32[4,32,128]{2,1,0:T(8,128)S(1)}, u32[]{:S(2)}, u32[]{:S(2)}) collective-permute-start(f32[4,32,128]{2,1,0:T(8,128)S(1)} %get-tuple-element.67), channel_id=1, source_target_pairs={{0,1},{1,0},{2,3},{3,2},{4,5},{5,4},{6,7},{7,6},{8,9},{9,8},{10,11... | collective-permute-start | bytes 196616 | tf_op jit(solution)/shard_map/ppermute | solution.py:31
  5.3 4.4 %collective-permute-start.1 = (f32[4,32,128]{2,1,0:T(8,128)S(1)}, f32[4,32,128]{2,1,0:T(8,128)S(1)}, u32[]{:S(2)}, u32[]{:S(2)}) collective-permute-start(f32[4,32,128]{2,1,0:T(8,128)S(1)} %get-tuple-element.68), channel_id=1, source_target_pairs={{0,8},{1,9},{2,10},{3,11},{4,12},{5,13},{6,14},{7,15},{8,16},{9,17... | collective-permute-start | bytes 196616 | tf_op jit(solution)/shard_map/ppermute | solution.py:31
  5.3 4.6 %collective-permute-start.2 = (f32[4,32,128]{2,1,0:T(8,128)S(1)}, f32[4,32,128]{2,1,0:T(8,128)S(1)}, u32[]{:S(2)}, u32[]{:S(2)}) collective-permute-start(f32[4,32,128]{2,1,0:T(8,128)S(1)} %get-tuple-element.69), channel_id=1, source_target_pairs={{0,9},{1,8},{2,11},{3,10},{4,13},{5,12},{6,15},{7,14},{8,17},{9,16... | collective-permute-start | bytes 196616 | tf_op jit(solution)/shard_map/ppermute | solution.py:31
  7.0 5.5 %collective-permute-start.3 = (f32[2,32,128]{2,1,0:T(8,128)S(1)}, f32[2,32,128]{2,1,0:T(8,128)S(1)}, u32[]{:S(2)}, u32[]{:S(2)}) collective-permute-start(f32[2,32,128]{2,1,0:T(8,128)S(1)} %get-tuple-element.74), channel_id=1, source_target_pairs={{0,4},{1,5},{2,6},{3,7},{4,0},{5,1},{6,2},{7,3},{8,12},{9,13},{10,... | collective-permute-start | bytes 98312 | tf_op jit(solution)/shard_map/ppermute | solution.py:31
  9.9 6.0 %collective-permute-start.4 = (f32[3,32,128]{2,1,0:T(8,128)S(1)}, f32[3,32,128]{2,1,0:T(8,128)S(1)}, u32[]{:S(2)}, u32[]{:S(2)}) collective-permute-start(f32[3,32,128]{2,1,0:T(8,128)S(1)} %pad_maximum_fusion), channel_id=1, source_target_pairs={{0,4},{1,5},{2,6},{3,7},{4,0},{5,1},{6,2},{7,3},{8,12},{9,13},{10,... | collective-permute-start | bytes 147464 | tf_op jit(solution)/shard_map/ppermute | solution.py:31
  12.6 7.5 %collective-permute-start.6 = (f32[5,32,128]{2,1,0:T(8,128)S(1)}, f32[5,32,128]{2,1,0:T(8,128)S(1)}, u32[]{:S(2)}, u32[]{:S(2)}) collective-permute-start(f32[5,32,128]{2,1,0:T(8,128)S(1)} %constant_dynamic-update-slice_fusion), channel_id=1, source_target_pairs={{0,2},{1,3},{2,0},{3,1},{4,6},{5,7},{6,4},{7,5},{8,10},{9,11},{10,... | collective-permute-start | bytes 245768 | tf_op jit(solution)/shard_map/ppermute | solution.py:31
  14.2 5.9 %collective-permute-start.5 = (f32[3,32,128]{2,1,0:T(8,128)S(1)}, f32[3,32,128]{2,1,0:T(8,128)S(1)}, u32[]{:S(2)}, u32[]{:S(2)}) collective-permute-start(f32[3,32,128]{2,1,0:T(8,128)S(1)} %pad_maximum_fusion.1), channel_id=1, source_target_pairs={{0,6},{1,7},{2,4},{3,5},{4,2},{5,3},{6,0},{7,1},{8,14},{9,15},{10,... | collective-permute-start | bytes 147464 | tf_op jit(solution)/shard_map/ppermute | solution.py:31
  21.2 4.3 %collective-permute-start.7 = (f32[4,32,128]{2,1,0:T(8,128)S(1)}, f32[4,32,128]{2,1,0:T(8,128)S(1)}, u32[]{:S(2)}, u32[]{:S(2)}) collective-permute-start(f32[4,32,128]{2,1,0:T(8,128)S(1)} %get-tuple-element.76), channel_id=1, source_target_pairs={{0,1},{1,0},{2,3},{3,2},{4,5},{5,4},{6,7},{7,6},{8,9},{9,8},{10,11... | collective-permute-start | bytes 196616 | tf_op jit(solution)/shard_map/ppermute | solution.py:31
  22.5 3.7 %collective-permute-start.8 = (f32[4,32,128]{2,1,0:T(8,128)S(1)}, f32[4,32,128]{2,1,0:T(8,128)S(1)}, u32[]{:S(2)}, u32[]{:S(2)}) collective-permute-start(f32[4,32,128]{2,1,0:T(8,128)S(1)} %get-tuple-element.77), channel_id=1, source_target_pairs={{0,8},{1,9},{2,10},{3,11},{4,12},{5,13},{6,14},{7,15},{8,16},{9,17... | collective-permute-start | bytes 196616 | tf_op jit(solution)/shard_map/ppermute | solution.py:31
  22.5 4.7 %collective-permute-start.9 = (f32[4,32,128]{2,1,0:T(8,128)S(1)}, f32[4,32,128]{2,1,0:T(8,128)S(1)}, u32[]{:S(2)}, u32[]{:S(2)}) collective-permute-start(f32[4,32,128]{2,1,0:T(8,128)S(1)} %get-tuple-element.78), channel_id=1, source_target_pairs={{0,9},{1,8},{2,11},{3,10},{4,13},{5,12},{6,15},{7,14},{8,17},{9,16... | collective-permute-start | bytes 196616 | tf_op jit(solution)/shard_map/ppermute | solution.py:31
  24.5 4.8 %collective-permute-start.10 = (f32[2,32,128]{2,1,0:T(8,128)S(1)}, f32[2,32,128]{2,1,0:T(8,128)S(1)}, u32[]{:S(2)}, u32[]{:S(2)}) collective-permute-start(f32[2,32,128]{2,1,0:T(8,128)S(1)} %get-tuple-element.83), channel_id=1, source_target_pairs={{0,4},{1,5},{2,6},{3,7},{4,0},{5,1},{6,2},{7,3},{8,12},{9,13},{10,... | collective-permute-start | bytes 98312 | tf_op jit(solution)/shard_map/ppermute | solution.py:31
  27.2 5.5 %collective-permute-start.11 = (f32[3,32,128]{2,1,0:T(8,128)S(1)}, f32[3,32,128]{2,1,0:T(8,128)S(1)}, u32[]{:S(2)}, u32[]{:S(2)}) collective-permute-start(f32[3,32,128]{2,1,0:T(8,128)S(1)} %pad_maximum_fusion.2), channel_id=1, source_target_pairs={{0,4},{1,5},{2,6},{3,7},{4,0},{5,1},{6,2},{7,3},{8,12},{9,13},{10,... | collective-permute-start | bytes 147464 | tf_op jit(solution)/shard_map/ppermute | solution.py:31
  29.3 6.4 %collective-permute-start.13 = (f32[5,32,128]{2,1,0:T(8,128)S(1)}, f32[5,32,128]{2,1,0:T(8,128)S(1)}, u32[]{:S(2)}, u32[]{:S(2)}) collective-permute-start(f32[5,32,128]{2,1,0:T(8,128)S(1)} %constant_dynamic-update-slice_fusion.5), channel_id=1, source_target_pairs={{0,2},{1,3},{2,0},{3,1},{4,6},{5,7},{6,4},{7,5},{8,10},{9,11},{10,... | collective-permute-start | bytes 245768 | tf_op jit(solution)/shard_map/ppermute | solution.py:31
  29.8 5.9 %collective-permute-start.12 = (f32[3,32,128]{2,1,0:T(8,128)S(1)}, f32[3,32,128]{2,1,0:T(8,128)S(1)}, u32[]{:S(2)}, u32[]{:S(2)}) collective-permute-start(f32[3,32,128]{2,1,0:T(8,128)S(1)} %pad_maximum_fusion.3), channel_id=1, source_target_pairs={{0,6},{1,7},{2,4},{3,5},{4,2},{5,3},{6,0},{7,1},{8,14},{9,15},{10,... | collective-permute-start | bytes 147464 | tf_op jit(solution)/shard_map/ppermute | solution.py:31
  36.8 4.3 %collective-permute-start.14 = (f32[4,32,128]{2,1,0:T(8,128)S(1)}, f32[4,32,128]{2,1,0:T(8,128)S(1)}, u32[]{:S(2)}, u32[]{:S(2)}) collective-permute-start(f32[4,32,128]{2,1,0:T(8,128)S(1)} %get-tuple-element.85), channel_id=1, source_target_pairs={{0,1},{1,0},{2,3},{3,2},{4,5},{5,4},{6,7},{7,6},{8,9},{9,8},{10,11... | collective-permute-start | bytes 196616 | tf_op jit(solution)/shard_map/ppermute | solution.py:31
  37.6 4.6 %collective-permute-start.16 = (f32[4,32,128]{2,1,0:T(8,128)S(1)}, f32[4,32,128]{2,1,0:T(8,128)S(1)}, u32[]{:S(2)}, u32[]{:S(2)}) collective-permute-start(f32[4,32,128]{2,1,0:T(8,128)S(1)} %get-tuple-element.87), channel_id=1, source_target_pairs={{0,9},{1,8},{2,11},{3,10},{4,13},{5,12},{6,15},{7,14},{8,17},{9,16... | collective-permute-start | bytes 196616 | tf_op jit(solution)/shard_map/ppermute | solution.py:31
  39.2 5.2 %collective-permute-start.17 = (f32[2,32,128]{2,1,0:T(8,128)S(1)}, f32[2,32,128]{2,1,0:T(8,128)S(1)}, u32[]{:S(2)}, u32[]{:S(2)}) collective-permute-start(f32[2,32,128]{2,1,0:T(8,128)S(1)} %get-tuple-element.92), channel_id=1, source_target_pairs={{0,4},{1,5},{2,6},{3,7},{4,0},{5,1},{6,2},{7,3},{8,12},{9,13},{10,... | collective-permute-start | bytes 98312 | tf_op jit(solution)/shard_map/ppermute | solution.py:31
  42.2 6.0 %collective-permute-start.18 = (f32[3,32,128]{2,1,0:T(8,128)S(1)}, f32[3,32,128]{2,1,0:T(8,128)S(1)}, u32[]{:S(2)}, u32[]{:S(2)}) collective-permute-start(f32[3,32,128]{2,1,0:T(8,128)S(1)} %pad_maximum_fusion.4), channel_id=1, source_target_pairs={{0,4},{1,5},{2,6},{3,7},{4,0},{5,1},{6,2},{7,3},{8,12},{9,13},{10,... | collective-permute-start | bytes 147464 | tf_op jit(solution)/shard_map/ppermute | solution.py:31
  44.3 6.4 %collective-permute-start.20 = (f32[5,32,128]{2,1,0:T(8,128)S(1)}, f32[5,32,128]{2,1,0:T(8,128)S(1)}, u32[]{:S(2)}, u32[]{:S(2)}) collective-permute-start(f32[5,32,128]{2,1,0:T(8,128)S(1)} %constant_dynamic-update-slice_fusion.10), channel_id=1, source_target_pairs={{0,2},{1,3},{2,0},{3,1},{4,6},{5,7},{6,4},{7,5},{8,10},{9,11},{10,... | collective-permute-start | bytes 245768 | tf_op jit(solution)/shard_map/ppermute | solution.py:31
  44.8 5.9 %collective-permute-start.19 = (f32[3,32,128]{2,1,0:T(8,128)S(1)}, f32[3,32,128]{2,1,0:T(8,128)S(1)}, u32[]{:S(2)}, u32[]{:S(2)}) collective-permute-start(f32[3,32,128]{2,1,0:T(8,128)S(1)} %pad_maximum_fusion.5), channel_id=1, source_target_pairs={{0,6},{1,7},{2,4},{3,5},{4,2},{5,3},{6,0},{7,1},{8,14},{9,15},{10,... | collective-permute-start | bytes 147464 | tf_op jit(solution)/shard_map/ppermute | solution.py:31
  51.9 4.3 %collective-permute-start.21 = (f32[4,32,128]{2,1,0:T(8,128)S(1)}, f32[4,32,128]{2,1,0:T(8,128)S(1)}, u32[]{:S(2)}, u32[]{:S(2)}) collective-permute-start(f32[4,32,128]{2,1,0:T(8,128)S(1)} %get-tuple-element.94), channel_id=1, source_target_pairs={{0,1},{1,0},{2,3},{3,2},{4,5},{5,4},{6,7},{7,6},{8,9},{9,8},{10,11... | collective-permute-start | bytes 196616 | tf_op jit(solution)/shard_map/ppermute | solution.py:31
  53.2 4.6 %collective-permute-start.23 = (f32[4,32,128]{2,1,0:T(8,128)S(1)}, f32[4,32,128]{2,1,0:T(8,128)S(1)}, u32[]{:S(2)}, u32[]{:S(2)}) collective-permute-start(f32[4,32,128]{2,1,0:T(8,128)S(1)} %get-tuple-element.96), channel_id=1, source_target_pairs={{0,9},{1,8},{2,11},{3,10},{4,13},{5,12},{6,15},{7,14},{8,17},{9,16... | collective-permute-start | bytes 196616 | tf_op jit(solution)/shard_map/ppermute | solution.py:31
  55.1 4.8 %collective-permute-start.24 = (f32[2,32,128]{2,1,0:T(8,128)S(1)}, f32[2,32,128]{2,1,0:T(8,128)S(1)}, u32[]{:S(2)}, u32[]{:S(2)}) collective-permute-start(f32[2,32,128]{2,1,0:T(8,128)S(1)} %get-tuple-element.101), channel_id=1, source_target_pairs={{0,4},{1,5},{2,6},{3,7},{4,0},{5,1},{6,2},{7,3},{8,12},{9,13},{10,... | collective-permute-start | bytes 98312 | tf_op jit(solution)/shard_map/ppermute | solution.py:31
  57.8 5.6 %collective-permute-start.25 = (f32[3,32,128]{2,1,0:T(8,128)S(1)}, f32[3,32,128]{2,1,0:T(8,128)S(1)}, u32[]{:S(2)}, u32[]{:S(2)}) collective-permute-start(f32[3,32,128]{2,1,0:T(8,128)S(1)} %pad_maximum_fusion.6), channel_id=1, source_target_pairs={{0,4},{1,5},{2,6},{3,7},{4,0},{5,1},{6,2},{7,3},{8,12},{9,13},{10,... | collective-permute-start | bytes 147464 | tf_op jit(solution)/shard_map/ppermute | solution.py:31
  60.0 6.4 %collective-permute-start.27 = (f32[5,32,128]{2,1,0:T(8,128)S(1)}, f32[5,32,128]{2,1,0:T(8,128)S(1)}, u32[]{:S(2)}, u32[]{:S(2)}) collective-permute-start(f32[5,32,128]{2,1,0:T(8,128)S(1)} %constant_dynamic-update-slice_fusion.15), channel_id=1, source_target_pairs={{0,2},{1,3},{2,0},{3,1},{4,6},{5,7},{6,4},{7,5},{8,10},{9,11},{10,... | collective-permute-start | bytes 245768 | tf_op jit(solution)/shard_map/ppermute | solution.py:31
  60.4 5.9 %collective-permute-start.26 = (f32[3,32,128]{2,1,0:T(8,128)S(1)}, f32[3,32,128]{2,1,0:T(8,128)S(1)}, u32[]{:S(2)}, u32[]{:S(2)}) collective-permute-start(f32[3,32,128]{2,1,0:T(8,128)S(1)} %pad_maximum_fusion.7), channel_id=1, source_target_pairs={{0,6},{1,7},{2,4},{3,5},{4,2},{5,3},{6,0},{7,1},{8,14},{9,15},{10,... | collective-permute-start | bytes 147464 | tf_op jit(solution)/shard_map/ppermute | solution.py:31
  67.4 4.3 %collective-permute-start.28 = (f32[4,32,128]{2,1,0:T(8,128)S(1)}, f32[4,32,128]{2,1,0:T(8,128)S(1)}, u32[]{:S(2)}, u32[]{:S(2)}) collective-permute-start(f32[4,32,128]{2,1,0:T(8,128)S(1)} %get-tuple-element.103), channel_id=1, source_target_pairs={{0,1},{1,0},{2,3},{3,2},{4,5},{5,4},{6,7},{7,6},{8,9},{9,8},{10,11... | collective-permute-start | bytes 196616 | tf_op jit(solution)/shard_map/ppermute | solution.py:31
  68.3 4.6 %collective-permute-start.30 = (f32[4,32,128]{2,1,0:T(8,128)S(1)}, f32[4,32,128]{2,1,0:T(8,128)S(1)}, u32[]{:S(2)}, u32[]{:S(2)}) collective-permute-start(f32[4,32,128]{2,1,0:T(8,128)S(1)} %get-tuple-element.105), channel_id=1, source_target_pairs={{0,9},{1,8},{2,11},{3,10},{4,13},{5,12},{6,15},{7,14},{8,17},{9,16... | collective-permute-start | bytes 196616 | tf_op jit(solution)/shard_map/ppermute | solution.py:31
  70.2 4.8 %collective-permute-start.31 = (f32[2,32,128]{2,1,0:T(8,128)S(1)}, f32[2,32,128]{2,1,0:T(8,128)S(1)}, u32[]{:S(2)}, u32[]{:S(2)}) collective-permute-start(f32[2,32,128]{2,1,0:T(8,128)S(1)} %get-tuple-element.110), channel_id=1, source_target_pairs={{0,4},{1,5},{2,6},{3,7},{4,0},{5,1},{6,2},{7,3},{8,12},{9,13},{10,... | collective-permute-start | bytes 98312 | tf_op jit(solution)/shard_map/ppermute | solution.py:31
  73.0 6.0 %collective-permute-start.32 = (f32[3,32,128]{2,1,0:T(8,128)S(1)}, f32[3,32,128]{2,1,0:T(8,128)S(1)}, u32[]{:S(2)}, u32[]{:S(2)}) collective-permute-start(f32[3,32,128]{2,1,0:T(8,128)S(1)} %pad_maximum_fusion.8), channel_id=1, source_target_pairs={{0,4},{1,5},{2,6},{3,7},{4,0},{5,1},{6,2},{7,3},{8,12},{9,13},{10,... | collective-permute-start | bytes 147464 | tf_op jit(solution)/shard_map/ppermute | solution.py:31
  75.0 6.5 %collective-permute-start.34 = (f32[5,32,128]{2,1,0:T(8,128)S(1)}, f32[5,32,128]{2,1,0:T(8,128)S(1)}, u32[]{:S(2)}, u32[]{:S(2)}) collective-permute-start(f32[5,32,128]{2,1,0:T(8,128)S(1)} %constant_dynamic-update-slice_fusion.20), channel_id=1, source_target_pairs={{0,2},{1,3},{2,0},{3,1},{4,6},{5,7},{6,4},{7,5},{8,10},{9,11},{10,... | collective-permute-start | bytes 245768 | tf_op jit(solution)/shard_map/ppermute | solution.py:31
  75.6 5.9 %collective-permute-start.33 = (f32[3,32,128]{2,1,0:T(8,128)S(1)}, f32[3,32,128]{2,1,0:T(8,128)S(1)}, u32[]{:S(2)}, u32[]{:S(2)}) collective-permute-start(f32[3,32,128]{2,1,0:T(8,128)S(1)} %pad_maximum_fusion.9), channel_id=1, source_target_pairs={{0,6},{1,7},{2,4},{3,5},{4,2},{5,3},{6,0},{7,1},{8,14},{9,15},{10,... | collective-permute-start | bytes 147464 | tf_op jit(solution)/shard_map/ppermute | solution.py:31
  (3 other events, 11.1 us)

commit v2 on v0

--- a/solution.py
+++ b/solution.py
@@ -139,9 +139,9 @@
         from_row = stepped(row, row_step, rows, back=True)
         for column_step in range(columns):
             source = from_row * columns + wrapped(column + columns - column_step, columns)
-            down = arrived[row_step].at[columns - 1 + column_step] if row_step else from_above[column_step].at[0]
+            down = arrived[row_step].at[column_step] if row_step else from_above[column_step].at[0]
             if column_step:
-                peer = arrived[row_step].at[column_step - 1] if row_step else over_columns[column_step].at[0]
+                peer = arrived[row_step].at[columns - 1 + column_step] if row_step else over_columns[column_step].at[0]
             else:
                 at, rest = row_step // half, row_step % half
                 peer = arrived[rest].at[2 * columns - 1 + at] if rest else own_column[at].at[0]
@@ -206,13 +206,13 @@
     for level in range(1, rounds + 1):
         over_columns = [moved(outs[c - 1], sections, rows, columns, (0, 0, c)) for c in range(1, columns)]
         from_above = [moved(outs[columns - 1 + c], sections, rows, columns, (1, 0, c)) for c in range(columns)]
-        over_columns, from_above = lax.optimization_barrier((over_columns, from_above))
+        from_above = lax.optimization_barrier(from_above)
         own_column = outs[2 * columns - 1 :]
         if half < rows:
             own_column[1] = moved(own_column[1], sections, rows, columns, (0, half, 0))
         arrived = []
         for step in range(rows - 1, 0, -1):
-            part = [value[step] for value in over_columns + from_above]
+            part = [value[step] for value in from_above + over_columns]
             if step < half:
                 part += [value[step] for value in own_column]
             arrived.append(moved(jnp.stack(part), sections, rows, columns, (0, step, 0)))

time: 83.2 us -> 89.2 us (1.072)
  waiting for transfers between devices: 26.1 us -> 29.7 us
  starting transfers between devices: 48 us -> 50.5 us
    ppermute x35, waiting for transfers between devices: 26.1 us -> 29.7 us  [moved(): return lax.ppermute(value, ('section', 'blk'), pairs)]
    ppermute x35, starting transfers between devices: 48 us -> 50.5 us  [moved(): return lax.ppermute(value, ('section', 'blk'), pairs)]
  transfers between devices with their start and end apart: 35 -> 35, of which waited for: 27 -> 20; matrix products, arithmetic and copies ran while one was open for 0% -> 0% of each run, Pallas kernels for 0% -> 0%
where the time goes in v2:
time: 89.2 us; the launch traced here: 89.1 us
  starting transfers between devices  50.5 us (57%)
  waiting for transfers between devices  29.7 us (33%)
  Pallas kernels  8.55 us (10%)
    ppermute x35, starting transfers between devices, moved(): return lax.ppermute(value, ('section', 'blk'), pairs)  50.5 us
    ppermute x35, waiting for transfers between devices, moved(): return lax.ppermute(value, ('section', 'blk'), pairs)  29.7 us
    pallas_call x5, Pallas kernels, shards(): pl.pallas_call(functools.partial(later_level, level, rows, columns), in_s...  6.3 us
    pallas_call x1, Pallas kernels, shards(): pl.pallas_call(functools.partial(first_level, rows, columns), in_specs=[h...  2.25 us
  transfers between devices with their start and end apart: 35, of which 20 were waited for; matrix products, arithmetic and copies ran while one was open for 0% of the time, Pallas kernels for 0%

profile of v2, /device:TPU:0, one launch (start us, length us, event | category | flops | bytes accessed | tf_op | source)
XLA Modules:
  0.0 89.1 jit_solution(1461124166388908832)
XLA Ops:
  0.0 2.3 %first_level.1 = (f32[129,32,128]{2,1,0:T(8,128)S(1)}, f32[48,32,32]{2,1,0:T(8,128)S(1)}, s32[294]{0:T(512)S(1)}, s32[5,1,8]{2,1,0:T(1,128)S(1)}, s32[5,1,8]{2,1...) custom-call(s32[48]{0:T(128)} %refs_0_.1, ...), custom_call_target="tpu_custom_call" | custom-call | tf_op jit(solution)/shard_map/first_level/pallas_call | solution.py:189
  2.8 3.7 %collective-permute-start.1 = (f32[4,32,128]{2,1,0:T(8,128)S(1)}, f32[4,32,128]{2,1,0:T(8,128)S(1)}, u32[]{:S(2)}, u32[]{:S(2)}) collective-permute-start(f32[4,32,128]{2,1,0:T(8,128)S(1)} %get-tuple-element.63), channel_id=1, source_target_pairs={{0,9},{1,8},{2,11},{3,10},{4,13},{5,12},{6,15},{7,14},{8,17},{9,16... | collective-permute-start | bytes 196616 | tf_op jit(solution)/shard_map/ppermute | solution.py:31
  6.5 2.6 %collective-permute-start.3 = (f32[2,32,128]{2,1,0:T(8,128)S(1)}, f32[2,32,128]{2,1,0:T(8,128)S(1)}, u32[]{:S(2)}, u32[]{:S(2)}) collective-permute-start(f32[2,32,128]{2,1,0:T(8,128)S(1)} %get-tuple-element.68), channel_id=1, source_target_pairs={{0,4},{1,5},{2,6},{3,7},{4,0},{5,1},{6,2},{7,3},{8,12},{9,13},{10,... | collective-permute-start | bytes 98312 | tf_op jit(solution)/shard_map/ppermute | solution.py:31
  9.6 3.7 %collective-permute-done.2.refs_2_ = f32[4,32,128]{2,1,0:T(8,128)S(1)} collective-permute-done((f32[4,32,128]{2,1,0:T(8,128)S(1)}, f32[4,32,128]{2,1,0:T(8,128)S(1)}, u32[]{:S(2)}, u32[]{:S(2)}) %collective-permute-start.2) | collective-permute-done | bytes 65568 | tf_op jit(solution)/shard_map/ppermute | solution.py:31
  13.4 1.4 %collective-permute-start.4 = (f32[3,32,128]{2,1,0:T(8,128)S(1)}, f32[3,32,128]{2,1,0:T(8,128)S(1)}, u32[]{:S(2)}, u32[]{:S(2)}) collective-permute-start(f32[3,32,128]{2,1,0:T(8,128)S(1)} %pad_maximum_fusion), channel_id=1, source_target_pairs={{0,6},{1,7},{2,4},{3,5},{4,2},{5,3},{6,0},{7,1},{8,14},{9,15},{10,... | collective-permute-start | bytes 147464 | tf_op jit(solution)/shard_map/ppermute | solution.py:31
  15.1 2.8 %collective-permute-start.5 = (f32[3,32,128]{2,1,0:T(8,128)S(1)}, f32[3,32,128]{2,1,0:T(8,128)S(1)}, u32[]{:S(2)}, u32[]{:S(2)}) collective-permute-start(f32[3,32,128]{2,1,0:T(8,128)S(1)} %pad_maximum_fusion.1), channel_id=1, source_target_pairs={{0,4},{1,5},{2,6},{3,7},{4,0},{5,1},{6,2},{7,3},{8,12},{9,13},{10,... | collective-permute-start | bytes 147464 | tf_op jit(solution)/shard_map/ppermute | solution.py:31
  17.9 1.5 %collective-permute-done.4.refs_5_ = f32[3,32,128]{2,1,0:T(8,128)S(1)} collective-permute-done((f32[3,32,128]{2,1,0:T(8,128)S(1)}, f32[3,32,128]{2,1,0:T(8,128)S(1)}, u32[]{:S(2)}, u32[]{:S(2)}) %collective-permute-start.4) | collective-permute-done | bytes 49184 | tf_op jit(solution)/shard_map/ppermute | solution.py:31
  22.6 2.1 %collective-permute-start.10 = (f32[2,32,128]{2,1,0:T(8,128)S(1)}, f32[2,32,128]{2,1,0:T(8,128)S(1)}, u32[]{:S(2)}, u32[]{:S(2)}) collective-permute-start(f32[2,32,128]{2,1,0:T(8,128)S(1)} %get-tuple-element.76), channel_id=1, source_target_pairs={{0,4},{1,5},{2,6},{3,7},{4,0},{5,1},{6,2},{7,3},{8,12},{9,13},{10,... | collective-permute-start | bytes 98312 | tf_op jit(solution)/shard_map/ppermute | solution.py:31
  24.8 1.5 %collective-permute-start.9 = (f32[4,32,128]{2,1,0:T(8,128)S(1)}, f32[4,32,128]{2,1,0:T(8,128)S(1)}, u32[]{:S(2)}, u32[]{:S(2)}) collective-permute-start(f32[4,32,128]{2,1,0:T(8,128)S(1)} %get-tuple-element.74), channel_id=1, source_target_pairs={{0,1},{1,0},{2,3},{3,2},{4,5},{5,4},{6,7},{7,6},{8,9},{9,8},{10,11... | collective-permute-start | bytes 196616 | tf_op jit(solution)/shard_map/ppermute | solution.py:31
  26.3 2.7 %collective-permute-done.9.refs_2_ = f32[4,32,128]{2,1,0:T(8,128)S(1)} collective-permute-done((f32[4,32,128]{2,1,0:T(8,128)S(1)}, f32[4,32,128]{2,1,0:T(8,128)S(1)}, u32[]{:S(2)}, u32[]{:S(2)}) %collective-permute-start.9) | collective-permute-done | bytes 65568 | tf_op jit(solution)/shard_map/ppermute | solution.py:31
  29.1 1.9 %collective-permute-start.11 = (f32[3,32,128]{2,1,0:T(8,128)S(1)}, f32[3,32,128]{2,1,0:T(8,128)S(1)}, u32[]{:S(2)}, u32[]{:S(2)}) collective-permute-start(f32[3,32,128]{2,1,0:T(8,128)S(1)} %pad_maximum_fusion.2), channel_id=1, source_target_pairs={{0,6},{1,7},{2,4},{3,5},{4,2},{5,3},{6,0},{7,1},{8,14},{9,15},{10,... | collective-permute-start | bytes 147464 | tf_op jit(solution)/shard_map/ppermute | solution.py:31
  31.0 2.6 %collective-permute-start.12 = (f32[3,32,128]{2,1,0:T(8,128)S(1)}, f32[3,32,128]{2,1,0:T(8,128)S(1)}, u32[]{:S(2)}, u32[]{:S(2)}) collective-permute-start(f32[3,32,128]{2,1,0:T(8,128)S(1)} %pad_maximum_fusion.3), channel_id=1, source_target_pairs={{0,4},{1,5},{2,6},{3,7},{4,0},{5,1},{6,2},{7,3},{8,12},{9,13},{10,... | collective-permute-start | bytes 147464 | tf_op jit(solution)/shard_map/ppermute | solution.py:31
  33.6 1.7 %collective-permute-done.11.refs_5_ = f32[3,32,128]{2,1,0:T(8,128)S(1)} collective-permute-done((f32[3,32,128]{2,1,0:T(8,128)S(1)}, f32[3,32,128]{2,1,0:T(8,128)S(1)}, u32[]{:S(2)}, u32[]{:S(2)}) %collective-permute-start.11) | collective-permute-done | bytes 49184 | tf_op jit(solution)/shard_map/ppermute | solution.py:31
  37.6 2.3 %collective-permute-start.15 = (f32[4,32,128]{2,1,0:T(8,128)S(1)}, f32[4,32,128]{2,1,0:T(8,128)S(1)}, u32[]{:S(2)}, u32[]{:S(2)}) collective-permute-start(f32[4,32,128]{2,1,0:T(8,128)S(1)} %get-tuple-element.79), channel_id=1, source_target_pairs={{0,9},{1,8},{2,11},{3,10},{4,13},{5,12},{6,15},{7,14},{8,17},{9,16... | collective-permute-start | bytes 196616 | tf_op jit(solution)/shard_map/ppermute | solution.py:31
  39.9 2.5 %collective-permute-start.17 = (f32[2,32,128]{2,1,0:T(8,128)S(1)}, f32[2,32,128]{2,1,0:T(8,128)S(1)}, u32[]{:S(2)}, u32[]{:S(2)}) collective-permute-start(f32[2,32,128]{2,1,0:T(8,128)S(1)} %get-tuple-element.84), channel_id=1, source_target_pairs={{0,4},{1,5},{2,6},{3,7},{4,0},{5,1},{6,2},{7,3},{8,12},{9,13},{10,... | collective-permute-start | bytes 98312 | tf_op jit(solution)/shard_map/ppermute | solution.py:31
  43.0 3.7 %collective-permute-done.16.refs_2_ = f32[4,32,128]{2,1,0:T(8,128)S(1)} collective-permute-done((f32[4,32,128]{2,1,0:T(8,128)S(1)}, f32[4,32,128]{2,1,0:T(8,128)S(1)}, u32[]{:S(2)}, u32[]{:S(2)}) %collective-permute-start.16) | collective-permute-done | bytes 65568 | tf_op jit(solution)/shard_map/ppermute | solution.py:31
  46.7 1.4 %collective-permute-start.18 = (f32[3,32,128]{2,1,0:T(8,128)S(1)}, f32[3,32,128]{2,1,0:T(8,128)S(1)}, u32[]{:S(2)}, u32[]{:S(2)}) collective-permute-start(f32[3,32,128]{2,1,0:T(8,128)S(1)} %pad_maximum_fusion.4), channel_id=1, source_target_pairs={{0,6},{1,7},{2,4},{3,5},{4,2},{5,3},{6,0},{7,1},{8,14},{9,15},{10,... | collective-permute-start | bytes 147464 | tf_op jit(solution)/shard_map/ppermute | solution.py:31
  48.3 3.0 %collective-permute-start.19 = (f32[3,32,128]{2,1,0:T(8,128)S(1)}, f32[3,32,128]{2,1,0:T(8,128)S(1)}, u32[]{:S(2)}, u32[]{:S(2)}) collective-permute-start(f32[3,32,128]{2,1,0:T(8,128)S(1)} %pad_maximum_fusion.5), channel_id=1, source_target_pairs={{0,4},{1,5},{2,6},{3,7},{4,0},{5,1},{6,2},{7,3},{8,12},{9,13},{10,... | collective-permute-start | bytes 147464 | tf_op jit(solution)/shard_map/ppermute | solution.py:31
  51.3 1.5 %collective-permute-done.18.refs_5_ = f32[3,32,128]{2,1,0:T(8,128)S(1)} collective-permute-done((f32[3,32,128]{2,1,0:T(8,128)S(1)}, f32[3,32,128]{2,1,0:T(8,128)S(1)}, u32[]{:S(2)}, u32[]{:S(2)}) %collective-permute-start.18) | collective-permute-done | bytes 49184 | tf_op jit(solution)/shard_map/ppermute | solution.py:31
  56.0 2.1 %collective-permute-start.24 = (f32[2,32,128]{2,1,0:T(8,128)S(1)}, f32[2,32,128]{2,1,0:T(8,128)S(1)}, u32[]{:S(2)}, u32[]{:S(2)}) collective-permute-start(f32[2,32,128]{2,1,0:T(8,128)S(1)} %get-tuple-element.92), channel_id=1, source_target_pairs={{0,4},{1,5},{2,6},{3,7},{4,0},{5,1},{6,2},{7,3},{8,12},{9,13},{10,... | collective-permute-start | bytes 98312 | tf_op jit(solution)/shard_map/ppermute | solution.py:31
  58.2 1.5 %collective-permute-start.23 = (f32[4,32,128]{2,1,0:T(8,128)S(1)}, f32[4,32,128]{2,1,0:T(8,128)S(1)}, u32[]{:S(2)}, u32[]{:S(2)}) collective-permute-start(f32[4,32,128]{2,1,0:T(8,128)S(1)} %get-tuple-element.90), channel_id=1, source_target_pairs={{0,1},{1,0},{2,3},{3,2},{4,5},{5,4},{6,7},{7,6},{8,9},{9,8},{10,11... | collective-permute-start | bytes 196616 | tf_op jit(solution)/shard_map/ppermute | solution.py:31
  59.7 2.8 %collective-permute-done.23.refs_2_ = f32[4,32,128]{2,1,0:T(8,128)S(1)} collective-permute-done((f32[4,32,128]{2,1,0:T(8,128)S(1)}, f32[4,32,128]{2,1,0:T(8,128)S(1)}, u32[]{:S(2)}, u32[]{:S(2)}) %collective-permute-start.23) | collective-permute-done | bytes 65568 | tf_op jit(solution)/shard_map/ppermute | solution.py:31
  62.5 1.8 %collective-permute-start.25 = (f32[3,32,128]{2,1,0:T(8,128)S(1)}, f32[3,32,128]{2,1,0:T(8,128)S(1)}, u32[]{:S(2)}, u32[]{:S(2)}) collective-permute-start(f32[3,32,128]{2,1,0:T(8,128)S(1)} %pad_maximum_fusion.6), channel_id=1, source_target_pairs={{0,6},{1,7},{2,4},{3,5},{4,2},{5,3},{6,0},{7,1},{8,14},{9,15},{10,... | collective-permute-start | bytes 147464 | tf_op jit(solution)/shard_map/ppermute | solution.py:31
  64.4 2.6 %collective-permute-start.26 = (f32[3,32,128]{2,1,0:T(8,128)S(1)}, f32[3,32,128]{2,1,0:T(8,128)S(1)}, u32[]{:S(2)}, u32[]{:S(2)}) collective-permute-start(f32[3,32,128]{2,1,0:T(8,128)S(1)} %pad_maximum_fusion.7), channel_id=1, source_target_pairs={{0,4},{1,5},{2,6},{3,7},{4,0},{5,1},{6,2},{7,3},{8,12},{9,13},{10,... | collective-permute-start | bytes 147464 | tf_op jit(solution)/shard_map/ppermute | solution.py:31
  67.0 1.7 %collective-permute-done.25.refs_5_ = f32[3,32,128]{2,1,0:T(8,128)S(1)} collective-permute-done((f32[3,32,128]{2,1,0:T(8,128)S(1)}, f32[3,32,128]{2,1,0:T(8,128)S(1)}, u32[]{:S(2)}, u32[]{:S(2)}) %collective-permute-start.25) | collective-permute-done | bytes 49184 | tf_op jit(solution)/shard_map/ppermute | solution.py:31
  71.0 2.3 %collective-permute-start.29 = (f32[4,32,128]{2,1,0:T(8,128)S(1)}, f32[4,32,128]{2,1,0:T(8,128)S(1)}, u32[]{:S(2)}, u32[]{:S(2)}) collective-permute-start(f32[4,32,128]{2,1,0:T(8,128)S(1)} %get-tuple-element.95), channel_id=1, source_target_pairs={{0,9},{1,8},{2,11},{3,10},{4,13},{5,12},{6,15},{7,14},{8,17},{9,16... | collective-permute-start | bytes 196616 | tf_op jit(solution)/shard_map/ppermute | solution.py:31
  73.3 2.5 %collective-permute-start.31 = (f32[2,32,128]{2,1,0:T(8,128)S(1)}, f32[2,32,128]{2,1,0:T(8,128)S(1)}, u32[]{:S(2)}, u32[]{:S(2)}) collective-permute-start(f32[2,32,128]{2,1,0:T(8,128)S(1)} %get-tuple-element.100), channel_id=1, source_target_pairs={{0,4},{1,5},{2,6},{3,7},{4,0},{5,1},{6,2},{7,3},{8,12},{9,13},{10,... | collective-permute-start | bytes 98312 | tf_op jit(solution)/shard_map/ppermute | solution.py:31
  76.4 3.7 %collective-permute-done.30.refs_2_ = f32[4,32,128]{2,1,0:T(8,128)S(1)} collective-permute-done((f32[4,32,128]{2,1,0:T(8,128)S(1)}, f32[4,32,128]{2,1,0:T(8,128)S(1)}, u32[]{:S(2)}, u32[]{:S(2)}) %collective-permute-start.30) | collective-permute-done | bytes 65568 | tf_op jit(solution)/shard_map/ppermute | solution.py:31
  80.1 1.4 %collective-permute-start.32 = (f32[3,32,128]{2,1,0:T(8,128)S(1)}, f32[3,32,128]{2,1,0:T(8,128)S(1)}, u32[]{:S(2)}, u32[]{:S(2)}) collective-permute-start(f32[3,32,128]{2,1,0:T(8,128)S(1)} %pad_maximum_fusion.8), channel_id=1, source_target_pairs={{0,6},{1,7},{2,4},{3,5},{4,2},{5,3},{6,0},{7,1},{8,14},{9,15},{10,... | collective-permute-start | bytes 147464 | tf_op jit(solution)/shard_map/ppermute | solution.py:31
  81.6 3.0 %collective-permute-start.33 = (f32[3,32,128]{2,1,0:T(8,128)S(1)}, f32[3,32,128]{2,1,0:T(8,128)S(1)}, u32[]{:S(2)}, u32[]{:S(2)}) collective-permute-start(f32[3,32,128]{2,1,0:T(8,128)S(1)} %pad_maximum_fusion.9), channel_id=1, source_target_pairs={{0,4},{1,5},{2,6},{3,7},{4,0},{5,1},{6,2},{7,3},{8,12},{9,13},{10,... | collective-permute-start | bytes 147464 | tf_op jit(solution)/shard_map/ppermute | solution.py:31
  84.7 1.5 %collective-permute-done.32.refs_5_ = f32[3,32,128]{2,1,0:T(8,128)S(1)} collective-permute-done((f32[3,32,128]{2,1,0:T(8,128)S(1)}, f32[3,32,128]{2,1,0:T(8,128)S(1)}, u32[]{:S(2)}, u32[]{:S(2)}) %collective-permute-start.32) | collective-permute-done | bytes 49184 | tf_op jit(solution)/shard_map/ppermute | solution.py:31
  87.1 2.0 %later_level.9 = (f32[129,32,128]{2,1,0:T(8,128)S(1)}, f32[48,32,128]{2,1,0:T(8,128)}) custom-call(s32[294]{0:T(512)S(1)} %get-tuple-element.54.plan, s32[5,1,8]{2,1,0:T(1,128)S(1)} %get-tuple-element.55.peers, s32[5,1,8]{2,1,0:T(1,128)S(1)} %get-tuple-element.56.downs, s32[4,48]{1,0:T(4,128)S(1)} %get-tuple-element.57.slots, ...), custom_call_target="tpu_custom_call", output_to_operand_aliasing={{0}: (16, {})} | custom-call | tf_op jit(solution)/shard_map/later_level/pallas_call | solution.py:224
  (79 shorter events, 14.8 us)
Async XLA Ops:
  2.3 7.4 %collective-permute-start = (f32[4,32,128]{2,1,0:T(8,128)S(1)}, f32[4,32,128]{2,1,0:T(8,128)S(1)}, u32[]{:S(2)}, u32[]{:S(2)}) collective-permute-start(f32[4,32,128]{2,1,0:T(8,128)S(1)} %get-tuple-element.62), channel_id=1, source_target_pairs={{0,8},{1,9},{2,10},{3,11},{4,12},{5,13},{6,14},{7,15},{8,16},{9,17... | collective-permute-start | bytes 196616 | tf_op jit(solution)/shard_map/ppermute | solution.py:31
  2.8 6.9 %collective-permute-start.1 = (f32[4,32,128]{2,1,0:T(8,128)S(1)}, f32[4,32,128]{2,1,0:T(8,128)S(1)}, u32[]{:S(2)}, u32[]{:S(2)}) collective-permute-start(f32[4,32,128]{2,1,0:T(8,128)S(1)} %get-tuple-element.63), channel_id=1, source_target_pairs={{0,9},{1,8},{2,11},{3,10},{4,13},{5,12},{6,15},{7,14},{8,17},{9,16... | collective-permute-start | bytes 196616 | tf_op jit(solution)/shard_map/ppermute | solution.py:31
  6.5 8.3 %collective-permute-start.3 = (f32[2,32,128]{2,1,0:T(8,128)S(1)}, f32[2,32,128]{2,1,0:T(8,128)S(1)}, u32[]{:S(2)}, u32[]{:S(2)}) collective-permute-start(f32[2,32,128]{2,1,0:T(8,128)S(1)} %get-tuple-element.68), channel_id=1, source_target_pairs={{0,4},{1,5},{2,6},{3,7},{4,0},{5,1},{6,2},{7,3},{8,12},{9,13},{10,... | collective-permute-start | bytes 98312 | tf_op jit(solution)/shard_map/ppermute | solution.py:31
  9.1 4.3 %collective-permute-start.2 = (f32[4,32,128]{2,1,0:T(8,128)S(1)}, f32[4,32,128]{2,1,0:T(8,128)S(1)}, u32[]{:S(2)}, u32[]{:S(2)}) collective-permute-start(f32[4,32,128]{2,1,0:T(8,128)S(1)} %get-tuple-element.66), channel_id=1, source_target_pairs={{0,1},{1,0},{2,3},{3,2},{4,5},{5,4},{6,7},{7,6},{8,9},{9,8},{10,11... | collective-permute-start | bytes 196616 | tf_op jit(solution)/shard_map/ppermute | solution.py:31
  13.4 6.1 %collective-permute-start.4 = (f32[3,32,128]{2,1,0:T(8,128)S(1)}, f32[3,32,128]{2,1,0:T(8,128)S(1)}, u32[]{:S(2)}, u32[]{:S(2)}) collective-permute-start(f32[3,32,128]{2,1,0:T(8,128)S(1)} %pad_maximum_fusion), channel_id=1, source_target_pairs={{0,6},{1,7},{2,4},{3,5},{4,2},{5,3},{6,0},{7,1},{8,14},{9,15},{10,... | collective-permute-start | bytes 147464 | tf_op jit(solution)/shard_map/ppermute | solution.py:31
  14.8 5.6 %collective-permute-start.6 = (f32[5,32,128]{2,1,0:T(8,128)S(1)}, f32[5,32,128]{2,1,0:T(8,128)S(1)}, u32[]{:S(2)}, u32[]{:S(2)}) collective-permute-start(f32[5,32,128]{2,1,0:T(8,128)S(1)} %constant_dynamic-update-slice_fusion), channel_id=1, source_target_pairs={{0,2},{1,3},{2,0},{3,1},{4,6},{5,7},{6,4},{7,5},{8,10},{9,11},{10,... | collective-permute-start | bytes 245768 | tf_op jit(solution)/shard_map/ppermute | solution.py:31
  15.1 5.0 %collective-permute-start.5 = (f32[3,32,128]{2,1,0:T(8,128)S(1)}, f32[3,32,128]{2,1,0:T(8,128)S(1)}, u32[]{:S(2)}, u32[]{:S(2)}) collective-permute-start(f32[3,32,128]{2,1,0:T(8,128)S(1)} %pad_maximum_fusion.1), channel_id=1, source_target_pairs={{0,4},{1,5},{2,6},{3,7},{4,0},{5,1},{6,2},{7,3},{8,12},{9,13},{10,... | collective-permute-start | bytes 147464 | tf_op jit(solution)/shard_map/ppermute | solution.py:31
  21.4 4.9 %collective-permute-start.7 = (f32[4,32,128]{2,1,0:T(8,128)S(1)}, f32[4,32,128]{2,1,0:T(8,128)S(1)}, u32[]{:S(2)}, u32[]{:S(2)}) collective-permute-start(f32[4,32,128]{2,1,0:T(8,128)S(1)} %get-tuple-element.70), channel_id=1, source_target_pairs={{0,8},{1,9},{2,10},{3,11},{4,12},{5,13},{6,14},{7,15},{8,16},{9,17... | collective-permute-start | bytes 196616 | tf_op jit(solution)/shard_map/ppermute | solution.py:31
  21.5 4.8 %collective-permute-start.8 = (f32[4,32,128]{2,1,0:T(8,128)S(1)}, f32[4,32,128]{2,1,0:T(8,128)S(1)}, u32[]{:S(2)}, u32[]{:S(2)}) collective-permute-start(f32[4,32,128]{2,1,0:T(8,128)S(1)} %get-tuple-element.71), channel_id=1, source_target_pairs={{0,9},{1,8},{2,11},{3,10},{4,13},{5,12},{6,15},{7,14},{8,17},{9,16... | collective-permute-start | bytes 196616 | tf_op jit(solution)/shard_map/ppermute | solution.py:31
  22.6 8.3 %collective-permute-start.10 = (f32[2,32,128]{2,1,0:T(8,128)S(1)}, f32[2,32,128]{2,1,0:T(8,128)S(1)}, u32[]{:S(2)}, u32[]{:S(2)}) collective-permute-start(f32[2,32,128]{2,1,0:T(8,128)S(1)} %get-tuple-element.76), channel_id=1, source_target_pairs={{0,4},{1,5},{2,6},{3,7},{4,0},{5,1},{6,2},{7,3},{8,12},{9,13},{10,... | collective-permute-start | bytes 98312 | tf_op jit(solution)/shard_map/ppermute | solution.py:31
  24.8 4.3 %collective-permute-start.9 = (f32[4,32,128]{2,1,0:T(8,128)S(1)}, f32[4,32,128]{2,1,0:T(8,128)S(1)}, u32[]{:S(2)}, u32[]{:S(2)}) collective-permute-start(f32[4,32,128]{2,1,0:T(8,128)S(1)} %get-tuple-element.74), channel_id=1, source_target_pairs={{0,1},{1,0},{2,3},{3,2},{4,5},{5,4},{6,7},{7,6},{8,9},{9,8},{10,11... | collective-permute-start | bytes 196616 | tf_op jit(solution)/shard_map/ppermute | solution.py:31
  29.1 6.3 %collective-permute-start.11 = (f32[3,32,128]{2,1,0:T(8,128)S(1)}, f32[3,32,128]{2,1,0:T(8,128)S(1)}, u32[]{:S(2)}, u32[]{:S(2)}) collective-permute-start(f32[3,32,128]{2,1,0:T(8,128)S(1)} %pad_maximum_fusion.2), channel_id=1, source_target_pairs={{0,6},{1,7},{2,4},{3,5},{4,2},{5,3},{6,0},{7,1},{8,14},{9,15},{10,... | collective-permute-start | bytes 147464 | tf_op jit(solution)/shard_map/ppermute | solution.py:31
  30.9 5.5 %collective-permute-start.13 = (f32[5,32,128]{2,1,0:T(8,128)S(1)}, f32[5,32,128]{2,1,0:T(8,128)S(1)}, u32[]{:S(2)}, u32[]{:S(2)}) collective-permute-start(f32[5,32,128]{2,1,0:T(8,128)S(1)} %constant_dynamic-update-slice_fusion.5), channel_id=1, source_target_pairs={{0,2},{1,3},{2,0},{3,1},{4,6},{5,7},{6,4},{7,5},{8,10},{9,11},{10,... | collective-permute-start | bytes 245768 | tf_op jit(solution)/shard_map/ppermute | solution.py:31
  31.0 5.1 %collective-permute-start.12 = (f32[3,32,128]{2,1,0:T(8,128)S(1)}, f32[3,32,128]{2,1,0:T(8,128)S(1)}, u32[]{:S(2)}, u32[]{:S(2)}) collective-permute-start(f32[3,32,128]{2,1,0:T(8,128)S(1)} %pad_maximum_fusion.3), channel_id=1, source_target_pairs={{0,4},{1,5},{2,6},{3,7},{4,0},{5,1},{6,2},{7,3},{8,12},{9,13},{10,... | collective-permute-start | bytes 147464 | tf_op jit(solution)/shard_map/ppermute | solution.py:31
  37.5 5.5 %collective-permute-start.14 = (f32[4,32,128]{2,1,0:T(8,128)S(1)}, f32[4,32,128]{2,1,0:T(8,128)S(1)}, u32[]{:S(2)}, u32[]{:S(2)}) collective-permute-start(f32[4,32,128]{2,1,0:T(8,128)S(1)} %get-tuple-element.78), channel_id=1, source_target_pairs={{0,8},{1,9},{2,10},{3,11},{4,12},{5,13},{6,14},{7,15},{8,16},{9,17... | collective-permute-start | bytes 196616 | tf_op jit(solution)/shard_map/ppermute | solution.py:31
  37.6 5.4 %collective-permute-start.15 = (f32[4,32,128]{2,1,0:T(8,128)S(1)}, f32[4,32,128]{2,1,0:T(8,128)S(1)}, u32[]{:S(2)}, u32[]{:S(2)}) collective-permute-start(f32[4,32,128]{2,1,0:T(8,128)S(1)} %get-tuple-element.79), channel_id=1, source_target_pairs={{0,9},{1,8},{2,11},{3,10},{4,13},{5,12},{6,15},{7,14},{8,17},{9,16... | collective-permute-start | bytes 196616 | tf_op jit(solution)/shard_map/ppermute | solution.py:31
  39.9 8.2 %collective-permute-start.17 = (f32[2,32,128]{2,1,0:T(8,128)S(1)}, f32[2,32,128]{2,1,0:T(8,128)S(1)}, u32[]{:S(2)}, u32[]{:S(2)}) collective-permute-start(f32[2,32,128]{2,1,0:T(8,128)S(1)} %get-tuple-element.84), channel_id=1, source_target_pairs={{0,4},{1,5},{2,6},{3,7},{4,0},{5,1},{6,2},{7,3},{8,12},{9,13},{10,... | collective-permute-start | bytes 98312 | tf_op jit(solution)/shard_map/ppermute | solution.py:31
  46.7 6.1 %collective-permute-start.18 = (f32[3,32,128]{2,1,0:T(8,128)S(1)}, f32[3,32,128]{2,1,0:T(8,128)S(1)}, u32[]{:S(2)}, u32[]{:S(2)}) collective-permute-start(f32[3,32,128]{2,1,0:T(8,128)S(1)} %pad_maximum_fusion.4), channel_id=1, source_target_pairs={{0,6},{1,7},{2,4},{3,5},{4,2},{5,3},{6,0},{7,1},{8,14},{9,15},{10,... | collective-permute-start | bytes 147464 | tf_op jit(solution)/shard_map/ppermute | solution.py:31
  48.2 5.6 %collective-permute-start.20 = (f32[5,32,128]{2,1,0:T(8,128)S(1)}, f32[5,32,128]{2,1,0:T(8,128)S(1)}, u32[]{:S(2)}, u32[]{:S(2)}) collective-permute-start(f32[5,32,128]{2,1,0:T(8,128)S(1)} %constant_dynamic-update-slice_fusion.10), channel_id=1, source_target_pairs={{0,2},{1,3},{2,0},{3,1},{4,6},{5,7},{6,4},{7,5},{8,10},{9,11},{10,... | collective-permute-start | bytes 245768 | tf_op jit(solution)/shard_map/ppermute | solution.py:31
  48.3 5.1 %collective-permute-start.19 = (f32[3,32,128]{2,1,0:T(8,128)S(1)}, f32[3,32,128]{2,1,0:T(8,128)S(1)}, u32[]{:S(2)}, u32[]{:S(2)}) collective-permute-start(f32[3,32,128]{2,1,0:T(8,128)S(1)} %pad_maximum_fusion.5), channel_id=1, source_target_pairs={{0,4},{1,5},{2,6},{3,7},{4,0},{5,1},{6,2},{7,3},{8,12},{9,13},{10,... | collective-permute-start | bytes 147464 | tf_op jit(solution)/shard_map/ppermute | solution.py:31
  54.8 4.9 %collective-permute-start.21 = (f32[4,32,128]{2,1,0:T(8,128)S(1)}, f32[4,32,128]{2,1,0:T(8,128)S(1)}, u32[]{:S(2)}, u32[]{:S(2)}) collective-permute-start(f32[4,32,128]{2,1,0:T(8,128)S(1)} %get-tuple-element.86), channel_id=1, source_target_pairs={{0,8},{1,9},{2,10},{3,11},{4,12},{5,13},{6,14},{7,15},{8,16},{9,17... | collective-permute-start | bytes 196616 | tf_op jit(solution)/shard_map/ppermute | solution.py:31
  54.9 4.8 %collective-permute-start.22 = (f32[4,32,128]{2,1,0:T(8,128)S(1)}, f32[4,32,128]{2,1,0:T(8,128)S(1)}, u32[]{:S(2)}, u32[]{:S(2)}) collective-permute-start(f32[4,32,128]{2,1,0:T(8,128)S(1)} %get-tuple-element.87), channel_id=1, source_target_pairs={{0,9},{1,8},{2,11},{3,10},{4,13},{5,12},{6,15},{7,14},{8,17},{9,16... | collective-permute-start | bytes 196616 | tf_op jit(solution)/shard_map/ppermute | solution.py:31
  56.0 8.3 %collective-permute-start.24 = (f32[2,32,128]{2,1,0:T(8,128)S(1)}, f32[2,32,128]{2,1,0:T(8,128)S(1)}, u32[]{:S(2)}, u32[]{:S(2)}) collective-permute-start(f32[2,32,128]{2,1,0:T(8,128)S(1)} %get-tuple-element.92), channel_id=1, source_target_pairs={{0,4},{1,5},{2,6},{3,7},{4,0},{5,1},{6,2},{7,3},{8,12},{9,13},{10,... | collective-permute-start | bytes 98312 | tf_op jit(solution)/shard_map/ppermute | solution.py:31
  62.5 6.2 %collective-permute-start.25 = (f32[3,32,128]{2,1,0:T(8,128)S(1)}, f32[3,32,128]{2,1,0:T(8,128)S(1)}, u32[]{:S(2)}, u32[]{:S(2)}) collective-permute-start(f32[3,32,128]{2,1,0:T(8,128)S(1)} %pad_maximum_fusion.6), channel_id=1, source_target_pairs={{0,6},{1,7},{2,4},{3,5},{4,2},{5,3},{6,0},{7,1},{8,14},{9,15},{10,... | collective-permute-start | bytes 147464 | tf_op jit(solution)/shard_map/ppermute | solution.py:31
  64.3 5.5 %collective-permute-start.27 = (f32[5,32,128]{2,1,0:T(8,128)S(1)}, f32[5,32,128]{2,1,0:T(8,128)S(1)}, u32[]{:S(2)}, u32[]{:S(2)}) collective-permute-start(f32[5,32,128]{2,1,0:T(8,128)S(1)} %constant_dynamic-update-slice_fusion.15), channel_id=1, source_target_pairs={{0,2},{1,3},{2,0},{3,1},{4,6},{5,7},{6,4},{7,5},{8,10},{9,11},{10,... | collective-permute-start | bytes 245768 | tf_op jit(solution)/shard_map/ppermute | solution.py:31
  64.4 5.1 %collective-permute-start.26 = (f32[3,32,128]{2,1,0:T(8,128)S(1)}, f32[3,32,128]{2,1,0:T(8,128)S(1)}, u32[]{:S(2)}, u32[]{:S(2)}) collective-permute-start(f32[3,32,128]{2,1,0:T(8,128)S(1)} %pad_maximum_fusion.7), channel_id=1, source_target_pairs={{0,4},{1,5},{2,6},{3,7},{4,0},{5,1},{6,2},{7,3},{8,12},{9,13},{10,... | collective-permute-start | bytes 147464 | tf_op jit(solution)/shard_map/ppermute | solution.py:31
  70.9 5.5 %collective-permute-start.28 = (f32[4,32,128]{2,1,0:T(8,128)S(1)}, f32[4,32,128]{2,1,0:T(8,128)S(1)}, u32[]{:S(2)}, u32[]{:S(2)}) collective-permute-start(f32[4,32,128]{2,1,0:T(8,128)S(1)} %get-tuple-element.94), channel_id=1, source_target_pairs={{0,8},{1,9},{2,10},{3,11},{4,12},{5,13},{6,14},{7,15},{8,16},{9,17... | collective-permute-start | bytes 196616 | tf_op jit(solution)/shard_map/ppermute | solution.py:31
  71.0 5.4 %collective-permute-start.29 = (f32[4,32,128]{2,1,0:T(8,128)S(1)}, f32[4,32,128]{2,1,0:T(8,128)S(1)}, u32[]{:S(2)}, u32[]{:S(2)}) collective-permute-start(f32[4,32,128]{2,1,0:T(8,128)S(1)} %get-tuple-element.95), channel_id=1, source_target_pairs={{0,9},{1,8},{2,11},{3,10},{4,13},{5,12},{6,15},{7,14},{8,17},{9,16... | collective-permute-start | bytes 196616 | tf_op jit(solution)/shard_map/ppermute | solution.py:31
  73.3 8.2 %collective-permute-start.31 = (f32[2,32,128]{2,1,0:T(8,128)S(1)}, f32[2,32,128]{2,1,0:T(8,128)S(1)}, u32[]{:S(2)}, u32[]{:S(2)}) collective-permute-start(f32[2,32,128]{2,1,0:T(8,128)S(1)} %get-tuple-element.100), channel_id=1, source_target_pairs={{0,4},{1,5},{2,6},{3,7},{4,0},{5,1},{6,2},{7,3},{8,12},{9,13},{10,... | collective-permute-start | bytes 98312 | tf_op jit(solution)/shard_map/ppermute | solution.py:31
  80.1 6.1 %collective-permute-start.32 = (f32[3,32,128]{2,1,0:T(8,128)S(1)}, f32[3,32,128]{2,1,0:T(8,128)S(1)}, u32[]{:S(2)}, u32[]{:S(2)}) collective-permute-start(f32[3,32,128]{2,1,0:T(8,128)S(1)} %pad_maximum_fusion.8), channel_id=1, source_target_pairs={{0,6},{1,7},{2,4},{3,5},{4,2},{5,3},{6,0},{7,1},{8,14},{9,15},{10,... | collective-permute-start | bytes 147464 | tf_op jit(solution)/shard_map/ppermute | solution.py:31
  81.5 5.6 %collective-permute-start.34 = (f32[5,32,128]{2,1,0:T(8,128)S(1)}, f32[5,32,128]{2,1,0:T(8,128)S(1)}, u32[]{:S(2)}, u32[]{:S(2)}) collective-permute-start(f32[5,32,128]{2,1,0:T(8,128)S(1)} %constant_dynamic-update-slice_fusion.20), channel_id=1, source_target_pairs={{0,2},{1,3},{2,0},{3,1},{4,6},{5,7},{6,4},{7,5},{8,10},{9,11},{10,... | collective-permute-start | bytes 245768 | tf_op jit(solution)/shard_map/ppermute | solution.py:31
  81.6 5.1 %collective-permute-start.33 = (f32[3,32,128]{2,1,0:T(8,128)S(1)}, f32[3,32,128]{2,1,0:T(8,128)S(1)}, u32[]{:S(2)}, u32[]{:S(2)}) collective-permute-start(f32[3,32,128]{2,1,0:T(8,128)S(1)} %pad_maximum_fusion.9), channel_id=1, source_target_pairs={{0,4},{1,5},{2,6},{3,7},{4,0},{5,1},{6,2},{7,3},{8,12},{9,13},{10,... | collective-permute-start | bytes 147464 | tf_op jit(solution)/shard_map/ppermute | solution.py:31
  (3 other events, 12.8 us)
